TPU v7x, 32 devices: a whole 2x2x4 slice. The times are simulated.
32 devices in a mesh: groups: 2 (over y), az: 4 (over z), rad: 4 (over x, core).
Axes of the slice: x: 2, y: 2, z: 4, core: 2. Of those that a mesh axis runs over, the one named last changes fastest.
Arguments:
- density: float32 [256, 1024], P(('groups', 'rad'), 'az'), parts along dimension 0, may hold values from 0.5 to 1.5
- momentum: float32 [4, 128, 1024], P('groups', 'rad', 'az'), parts along dimension 0, may hold values from -1 to 1
- shear_shift: int32 [4], P('groups'), parts along dimension 0, may hold values from 0 to 1023
- shear_frac: float32 [4], P('groups'), parts along dimension 0, may hold values from 0 to 1
- advect_shift: int32 [256], P(('groups', 'rad')), parts along dimension 0, may hold values from 0 to 1023
- advect_frac: float32 [256], P(('groups', 'rad')), parts along dimension 0, may hold values from 0 to 1
- rotation: float32 [2], P('groups'), parts along dimension 0, may hold values from 0.5 to 2
Outputs:
- density_out: float32 [256, 1024], P(('groups', 'rad'), 'az'), parts along dimension 0
- momentum_out: float32 [4, 128, 1024], P('groups', 'rad', 'az'), parts along dimension 0
There are 2 independent parts, one for each index of `groups`. A program takes and returns all parts, laid end to end along the dimension named above; each array names one. Nothing has to cross between parts.
All inputs are finite; a program needn't handle non-finite values.
Results may differ from a plain program's by a relative error of at most 0.0003.
Values sent between devices are 32-bit elements; how exact they have to be, the bound alone decides.
No kernel may reach another device: no remote copies, remote signals or barrier semaphores. Data moves between devices by JAX's collectives and lax.ppermute only.
A program may use at most 64 MiB of HBM per device.

v0:
```python
import jax
import jax.numpy as jnp
from jax import lax
from jax.sharding import PartitionSpec as P

time_step = 0.12
sound_speed = 1.0


def passed_along(value, axis, steps):
    count = lax.axis_size(axis)
    pairs = [(source, (source + steps) % count) for source in range(count)]
    return lax.ppermute(value, axis, pairs)


def padded_2(block, sides, width):
    for axis, dim in sides:
        count = lax.axis_size(axis)
        forward = [(i, i + 1) for i in range(count - 1)]
        forward.append((count - 1, 0))
        backward = [(target, source) for source, target in forward]
        low = lax.ppermute(
            lax.slice_in_dim(block, block.shape[dim] - width, None, axis=dim), axis, forward
        )
        high = lax.ppermute(lax.slice_in_dim(block, 0, width, axis=dim), axis, backward)
        block = jnp.concatenate([low, block, high], axis=dim)
    return block


def minmod(first, second):
    return 0.5 * (jnp.sign(first) + jnp.sign(second)) * jnp.minimum(jnp.abs(first), jnp.abs(second))


def trimmed(array, lower, upper, direction):
    return lax.slice_in_dim(array, lower, array.shape[direction] - upper, axis=direction)


def physical(state):
    mass_flux = state[0] * state[1]
    fluxes = jnp.stack(
        [
            mass_flux,
            mass_flux * state[1] + sound_speed * sound_speed * state[0],
            mass_flux * state[2],
        ]
    )
    conserved = jnp.stack([state[0], state[0] * state[1], state[0] * state[2]])
    return (fluxes, conserved)


def face_flux(left_state, right_state):
    left_flux, left_cons = physical(left_state)
    right_flux, right_cons = physical(right_state)
    signal = jnp.maximum(jnp.abs(left_state[1]), jnp.abs(right_state[1])) + sound_speed
    return 0.5 * (left_flux + right_flux) - 0.5 * signal * (right_cons - left_cons)


def primitive(conserved, normal):
    return jnp.stack(
        [conserved[0], conserved[normal] / conserved[0], conserved[3 - normal] / conserved[0]]
    )


def sweep_axis(prims, direction):
    slopes = minmod(
        trimmed(prims, 1, 1, direction) - trimmed(prims, 0, 2, direction),
        trimmed(prims, 2, 0, direction) - trimmed(prims, 1, 1, direction),
    )
    left_state = trimmed(prims, 1, 2, direction) + 0.5 * trimmed(slopes, 0, 1, direction)
    right_state = trimmed(prims, 2, 1, direction) - 0.5 * trimmed(slopes, 1, 0, direction)
    fluxes = face_flux(left_state, right_state)
    return trimmed(fluxes, 1, 0, direction) - trimmed(fluxes, 0, 1, direction)


def strip_window(source, start, tile_width, fraction):
    window = lax.dynamic_slice_in_dim(source, start, tile_width + 1, source.ndim - 1)
    return (1.0 - fraction) * window[..., 1:] + fraction * window[..., :-1]


def row_barrel(rows, amounts, bit_count, sign):
    current = rows
    for level in range(bit_count):
        moved = jnp.roll(current, sign * 2**level, axis=2)
        taken = amounts // 2**level % 2 == 1
        current = jnp.where(taken[None, :, None], moved, current)
    return current


def sheared(strips, offset_cells, fraction):
    tile_width = strips.shape[3]
    total_cells = lax.axis_size("az") * tile_width
    backward = (total_cells - offset_cells - 1) % total_cells
    offsets = [offset_cells, backward]
    weights = [fraction, 1.0 - fraction]
    results = []
    offset_arr = jnp.stack(offsets)
    tiles = offset_arr // tile_width
    within = offset_arr % tile_width
    current = strips
    for level in range(lax.axis_size("az").bit_length() - 1):
        moved = passed_along(current, "az", 2**level)
        taken = tiles // 2**level % 2 == 1
        current = jnp.where(taken[:, None, None, None], moved, current)
    before = passed_along(current, "az", 1)
    joined = jnp.concatenate([before, current], axis=3)
    for side in range(2):
        start = tile_width - within[side] - 1
        results.append(strip_window(joined[side], start, tile_width, weights[side]))
    return jnp.stack(results)


def tendency(state, offset_cells, fraction, rotation):
    padded = padded_2(state, (("az", 2), ("rad", 1)), 2)
    columns = padded[:, :, 2:-2]
    strips = jnp.stack([columns[:, :2], columns[:, -2:]])
    ghosts = sheared(strips, offset_cells, fraction)
    radial = lax.axis_index("rad")
    lower_ghost = jnp.where(radial == 0, ghosts[0], columns[:, :2])
    upper_ghost = jnp.where(radial == lax.axis_size("rad") - 1, ghosts[1], columns[:, -2:])
    columns = jnp.concatenate([lower_ghost, columns[:, 2:-2], upper_ghost], axis=1)
    cycle_rows = padded[:, 2:-2, :]
    radial_div = sweep_axis(primitive(columns, 1), 1)
    azimuth_div = sweep_axis(primitive(cycle_rows, 2), 2)
    azimuth_div = jnp.stack([azimuth_div[0], azimuth_div[2], azimuth_div[1]])
    source = jnp.stack(
        [jnp.zeros_like(state[0]), 2.0 * rotation * state[2], -0.5 * rotation * state[1]]
    )
    return -(radial_div + azimuth_div) + source


def remap_rows(state, row_shift, row_frac):
    tile_width = state.shape[2]
    tiles = row_shift // tile_width
    within = row_shift % tile_width
    current = state
    for level in range(lax.axis_size("az").bit_length() - 1):
        moved = passed_along(current, "az", 2**level)
        taken = tiles // 2**level % 2 == 1
        current = jnp.where(taken[None, :, None], moved, current)
    before = passed_along(current, "az", 1)
    joined = jnp.concatenate([before, current], axis=2)
    lead = tile_width - within - 1
    aligned = row_barrel(joined, lead, tile_width.bit_length(), -1)
    weight = row_frac[None, :, None]
    return (1.0 - weight) * aligned[:, :, 1 : tile_width + 1] + weight * aligned[:, :, :tile_width]


def per_device(density, momentum, shear_shift, shear_frac, advect_shift, advect_frac, rotation):
    state = jnp.concatenate([density[None], momentum], axis=0)
    middle = state + time_step * tendency(state, shear_shift[0], shear_frac[0], rotation[0])
    final = 0.5 * state + 0.5 * (
        middle + time_step * tendency(middle, shear_shift[1], shear_frac[1], rotation[0])
    )
    remapped = remap_rows(final, advect_shift, advect_frac)
    return (remapped[0], remapped[1:])


def solution(mesh):
    in_specs = (
        P(("groups", "rad"), "az"),
        P("groups", "rad", "az"),
        P("groups"),
        P("groups"),
        P(("groups", "rad")),
        P(("groups", "rad")),
        P("groups"),
    )
    out_specs = (P(("groups", "rad"), "az"), P("groups", "rad", "az"))
    return jax.shard_map(
        per_device, mesh=mesh, in_specs=in_specs, out_specs=out_specs, check_vma=False
    )
```

profile of v0, /device:TPU:0, one launch (start us, length us, event | category | flops | bytes accessed | tf_op | source)
XLA Modules:
  0.0 92.7 jit_solution(8966657337533228687)
XLA Ops:
  0.6 0.9 fusion.35
  1.5 3.1 %collective-permute-start = (f32[3,32,2]{2,1,0:T(8,128)S(1)}, f32[3,32,2]{2,1,0:T(8,128)S(1)}, u32[]{:S(2)}, u32[]{:S(2)}) collective-permute-start(f32[3,32,2]{2,1,0:T(8,128)S(1)} %get-tuple-element.92), channel_id=1, source_target_pairs={{0,4},{4,8},{8,12},{12,0},{1,5},{5,9},{9,13},{13,1},{2,6},{6,10},{... | collective-permute-start | bytes 2312 | tf_op jit(solution)/shard_map/ppermute | solution.py:22
  4.6 2.1 %collective-permute-start.1 = (f32[3,32,2]{2,1,0:T(8,128)S(1)}, f32[3,32,2]{2,1,0:T(8,128)S(1)}, u32[]{:S(2)}, u32[]{:S(2)}) collective-permute-start(f32[3,32,2]{2,1,0:T(8,128)S(1)} %get-tuple-element.93), channel_id=1, source_target_pairs={{4,0},{8,4},{12,8},{0,12},{5,1},{9,5},{13,9},{1,13},{6,2},{10,6},{... | collective-permute-start | bytes 2312 | tf_op jit(solution)/shard_map/ppermute | solution.py:25
  6.7 0.6 fusion.89
  7.9 0.8 fusion.63
  8.7 0.7 fusion.90
  12.7 0.7 fusion.65
  13.5 0.6 fusion.87
  16.7 0.6 copy-done.3
  17.4 0.6 fusion.88
  20.1 0.7 copy-done.1
  20.7 0.1 pad_maximum_fusion.2
  20.9 0.2 minimum_multiply_fusion.1
  21.1 0.2 fusion.4
  21.3 0.1 pad_maximum_fusion.15
  21.4 0.7 collective-permute-start.3
  22.2 1.3 %collective-permute-done.3 = f32[3,2,260]{2,1,0:T(2,128)S(1)} collective-permute-done((f32[3,2,260]{2,1,0:T(2,128)S(1)}, f32[3,2,260]{2,1,0:T(2,128)S(1)}, u32[]{:S(2)}, u32[]{:S(2)}) %collective-permute-start.3) | collective-permute-done | bytes 6272 | tf_op jit(solution)/shard_map/ppermute | solution.py:25
  23.5 1.6 %collective-permute-done.2 = f32[3,2,260]{2,1,0:T(2,128)S(1)} collective-permute-done((f32[3,2,260]{2,1,0:T(2,128)S(1)}, f32[3,2,260]{2,1,0:T(2,128)S(1)}, u32[]{:S(2)}, u32[]{:S(2)}) %collective-permute-start.2) | collective-permute-done | bytes 6272 | tf_op jit(solution)/shard_map/ppermute | solution.py:22
  25.3 0.1 slice_subtract_fusion.10
  25.4 5.4 %collective-permute-done.4 = f32[2,3,2,256]{3,2,1,0:T(2,128)S(1)} collective-permute-done((f32[2,3,2,256]{3,2,1,0:T(2,128)S(1)}, f32[2,3,2,256]{3,2,1,0:T(2,128)S(1)}, u32[]{:S(2)}, u32[]{:S(2)}) %collective-permute-start.4) | collective-permute-done | bytes 12320 | tf_op jit(solution)/shard_map/ppermute | solution.py:13
  31.0 4.6 %collective-permute-done.5 = f32[2,3,2,256]{3,2,1,0:T(2,128)S(1)} collective-permute-done((f32[2,3,2,256]{3,2,1,0:T(2,128)S(1)}, f32[2,3,2,256]{3,2,1,0:T(2,128)S(1)}, u32[]{:S(2)}, u32[]{:S(2)}) %collective-permute-start.5) | collective-permute-done | bytes 12320 | tf_op jit(solution)/shard_map/ppermute | solution.py:13
  35.6 5.5 %collective-permute-done.6 = f32[2,3,2,256]{3,2,1,0:T(2,128)S(1)} collective-permute-done((f32[2,3,2,256]{3,2,1,0:T(2,128)S(1)}, f32[2,3,2,256]{3,2,1,0:T(2,128)S(1)}, u32[]{:S(2)}, u32[]{:S(2)}) %collective-permute-start.6) | collective-permute-done | bytes 12320 | tf_op jit(solution)/shard_map/ppermute | solution.py:13
  41.2 0.1 fusion.38
  41.3 0.7 fusion.48
  42.1 0.1 minimum_multiply_fusion.3
  42.6 3.8 %collective-permute-start.8 = (f32[3,32,2]{2,1,0:T(8,128)S(1)}, f32[3,32,2]{2,1,0:T(8,128)S(1)}, u32[]{:S(2)}, u32[]{:S(2)}) collective-permute-start(f32[3,32,2]{2,1,0:T(8,128)S(1)} %get-tuple-element.88), channel_id=1, source_target_pairs={{4,0},{8,4},{12,8},{0,12},{5,1},{9,5},{13,9},{1,13},{6,2},{10,6},{... | collective-permute-start | bytes 2312 | tf_op jit(solution)/shard_map/ppermute | solution.py:25
  46.4 2.1 %collective-permute-done.7 = f32[3,32,2]{2,1,0:T(8,128)S(1)} collective-permute-done((f32[3,32,2]{2,1,0:T(8,128)S(1)}, f32[3,32,2]{2,1,0:T(8,128)S(1)}, u32[]{:S(2)}, u32[]{:S(2)}) %collective-permute-start.7) | collective-permute-done | bytes 800 | tf_op jit(solution)/shard_map/ppermute | solution.py:22
  48.4 0.1 pad_maximum_fusion.4
  48.6 0.2 minimum_multiply_fusion
  48.8 0.2 fusion.2
  49.0 0.1 pad_maximum_fusion.13
  49.2 0.5 collective-permute-start.9
  49.8 0.8 collective-permute-done.10
  50.6 1.7 %collective-permute-done.9 = f32[3,2,260]{2,1,0:T(2,128)S(1)} collective-permute-done((f32[3,2,260]{2,1,0:T(2,128)S(1)}, f32[3,2,260]{2,1,0:T(2,128)S(1)}, u32[]{:S(2)}, u32[]{:S(2)}) %collective-permute-start.9) | collective-permute-done | bytes 6272 | tf_op jit(solution)/shard_map/ppermute | solution.py:22
  52.5 0.1 slice_subtract_fusion.8
  52.6 5.4 %collective-permute-done.11 = f32[2,3,2,256]{3,2,1,0:T(2,128)S(1)} collective-permute-done((f32[2,3,2,256]{3,2,1,0:T(2,128)S(1)}, f32[2,3,2,256]{3,2,1,0:T(2,128)S(1)}, u32[]{:S(2)}, u32[]{:S(2)}) %collective-permute-start.11) | collective-permute-done | bytes 12320 | tf_op jit(solution)/shard_map/ppermute | solution.py:13
  58.0 0.3 collective-permute-start.12
  58.3 4.3 %collective-permute-done.12 = f32[2,3,2,256]{3,2,1,0:T(2,128)S(1)} collective-permute-done((f32[2,3,2,256]{3,2,1,0:T(2,128)S(1)}, f32[2,3,2,256]{3,2,1,0:T(2,128)S(1)}, u32[]{:S(2)}, u32[]{:S(2)}) %collective-permute-start.12) | collective-permute-done | bytes 12320 | tf_op jit(solution)/shard_map/ppermute | solution.py:13
  62.7 5.5 %collective-permute-done.13 = f32[2,3,2,256]{3,2,1,0:T(2,128)S(1)} collective-permute-done((f32[2,3,2,256]{3,2,1,0:T(2,128)S(1)}, f32[2,3,2,256]{3,2,1,0:T(2,128)S(1)}, u32[]{:S(2)}, u32[]{:S(2)}) %collective-permute-start.13) | collective-permute-done | bytes 12320 | tf_op jit(solution)/shard_map/ppermute | solution.py:13
  68.3 0.7 fusion.46
  69.0 0.1 fusion.40
  69.3 0.1 minimum_multiply_fusion.2
  69.6 0.1 fusion.29
  69.7 6.5 %collective-permute-done.14 = f32[3,32,256]{2,1,0:T(8,128)S(1)} collective-permute-done((f32[3,32,256]{2,1,0:T(8,128)S(1)}, f32[3,32,256]{2,1,0:T(8,128)S(1)}, u32[]{:S(2)}, u32[]{:S(2)}) %collective-permute-start.14) | collective-permute-done | bytes 98336 | tf_op jit(solution)/shard_map/ppermute | solution.py:13
  76.4 6.5 %collective-permute-done.15 = f32[3,32,256]{2,1,0:T(8,128)S(1)} collective-permute-done((f32[3,32,256]{2,1,0:T(8,128)S(1)}, f32[3,32,256]{2,1,0:T(8,128)S(1)}, u32[]{:S(2)}, u32[]{:S(2)}) %collective-permute-start.15) | collective-permute-done | bytes 98336 | tf_op jit(solution)/shard_map/ppermute | solution.py:13
  83.0 0.6 copy-done.4
  83.6 5.8 %collective-permute-done.16 = f32[3,32,256]{2,1,0:T(8,128)S(1)} collective-permute-done((f32[3,32,256]{2,1,0:T(8,128)S(1)}, f32[3,32,256]{2,1,0:T(8,128)S(1)}, u32[]{:S(2)}, u32[]{:S(2)}) %collective-permute-start.16) | collective-permute-done | bytes 98336 | tf_op jit(solution)/shard_map/ppermute | solution.py:13
  89.4 0.1 fusion
  89.5 0.1 fusion.1
  89.6 0.1 slice.764
  89.8 0.1 maximum_select_fusion
  89.9 0.1 slice.766
  90.0 0.1 maximum_select_fusion.1
  90.1 0.1 slice.768
  90.2 0.1 maximum_select_fusion.2
  90.4 0.1 slice.770
  90.5 0.1 maximum_select_fusion.3
  90.6 0.1 slice.772
  90.7 0.1 maximum_select_fusion.4
  90.8 0.1 slice.774
  91.0 0.1 maximum_select_fusion.5
  91.3 0.1 fusion.22
  91.4 0.6 slice.783
  92.0 0.6 slice_bitcast_fusion
  (96 shorter events, 2.6 us)
Async XLA Ops:
  1.5 5.2 %copy-start.2 = (s32[2]{0:T(128)S(1)}, s32[2]{0:T(128)}, u32[]{:S(2)}) copy-start(s32[2]{0:T(128)} %param.9) | copy-start | bytes 28
  1.5 18.6 %collective-permute-start = (f32[3,32,2]{2,1,0:T(8,128)S(1)}, f32[3,32,2]{2,1,0:T(8,128)S(1)}, u32[]{:S(2)}, u32[]{:S(2)}) collective-permute-start(f32[3,32,2]{2,1,0:T(8,128)S(1)} %get-tuple-element.92), channel_id=1, source_target_pairs={{0,4},{4,8},{8,12},{12,0},{1,5},{5,9},{9,13},{13,1},{2,6},{6,10},{... | collective-permute-start | bytes 2312 | tf_op jit(solution)/shard_map/ppermute | solution.py:22
  4.6 15.5 %collective-permute-start.1 = (f32[3,32,2]{2,1,0:T(8,128)S(1)}, f32[3,32,2]{2,1,0:T(8,128)S(1)}, u32[]{:S(2)}, u32[]{:S(2)}) collective-permute-start(f32[3,32,2]{2,1,0:T(8,128)S(1)} %get-tuple-element.93), channel_id=1, source_target_pairs={{4,0},{8,4},{12,8},{0,12},{5,1},{9,5},{13,9},{1,13},{6,2},{10,6},{... | collective-permute-start | bytes 2312 | tf_op jit(solution)/shard_map/ppermute | solution.py:25
  7.9 12.1 %copy-start = (f32[2,32,256]{2,1,0:T(8,128)S(1)}, f32[2,32,256]{2,1,0:T(8,128)}, u32[]{:S(2)}) copy-start(f32[2,32,256]{2,1,0:T(8,128)} %param.8) | copy-start | bytes 196612
  16.7 0.7 copy-start.3
  19.3 0.7 copy-start.5
  20.0 0.8 copy-start.1
  21.4 2.1 %collective-permute-start.3 = (f32[3,2,260]{2,1,0:T(2,128)S(1)}, f32[3,2,260]{2,1,0:T(2,128)S(1)}, u32[]{:S(2)}, u32[]{:S(2)}) collective-permute-start(f32[3,2,260]{2,1,0:T(2,128)S(1)} %get-tuple-element.41), channel_id=1, source_target_pairs={{1,0},{2,1},{3,2},{0,3},{5,4},{6,5},{7,6},{4,7},{9,8},{10,9},{11,1... | collective-permute-start | bytes 18728 | tf_op jit(solution)/shard_map/ppermute | solution.py:25
  22.1 3.1 %collective-permute-start.2 = (f32[3,2,260]{2,1,0:T(2,128)S(1)}, f32[3,2,260]{2,1,0:T(2,128)S(1)}, u32[]{:S(2)}, u32[]{:S(2)}) collective-permute-start(f32[3,2,260]{2,1,0:T(2,128)S(1)} %get-tuple-element.40), channel_id=1, source_target_pairs={{0,1},{1,2},{2,3},{3,0},{4,5},{5,6},{6,7},{7,4},{8,9},{9,10},{10,1... | collective-permute-start | bytes 18728 | tf_op jit(solution)/shard_map/ppermute | solution.py:22
  25.2 5.6 %collective-permute-start.4 = (f32[2,3,2,256]{3,2,1,0:T(2,128)S(1)}, f32[2,3,2,256]{3,2,1,0:T(2,128)S(1)}, u32[]{:S(2)}, u32[]{:S(2)}) collective-permute-start(f32[2,3,2,256]{3,2,1,0:T(2,128)S(1)} %pad_maximum_fusion.10), channel_id=1, source_target_pairs={{0,4},{4,8},{8,12},{12,0},{1,5},{5,9},{9,13},{13,1},{2,6},{6,10},{... | collective-permute-start | bytes 36872 | tf_op jit(solution)/shard_map/ppermute | solution.py:13
  30.9 4.6 %collective-permute-start.5 = (f32[2,3,2,256]{3,2,1,0:T(2,128)S(1)}, f32[2,3,2,256]{3,2,1,0:T(2,128)S(1)}, u32[]{:S(2)}, u32[]{:S(2)}) collective-permute-start(f32[2,3,2,256]{3,2,1,0:T(2,128)S(1)} %broadcast_select_fusion.4), channel_id=1, source_target_pairs={{0,8},{4,12},{8,0},{12,4},{1,9},{5,13},{9,1},{13,5},{2,10},{6,14},... | collective-permute-start | bytes 36872 | tf_op jit(solution)/shard_map/ppermute | solution.py:13
  35.6 5.5 %collective-permute-start.6 = (f32[2,3,2,256]{3,2,1,0:T(2,128)S(1)}, f32[2,3,2,256]{3,2,1,0:T(2,128)S(1)}, u32[]{:S(2)}, u32[]{:S(2)}) collective-permute-start(f32[2,3,2,256]{3,2,1,0:T(2,128)S(1)} %broadcast_select_fusion.5), channel_id=1, source_target_pairs={{0,4},{4,8},{8,12},{12,0},{1,5},{5,9},{9,13},{13,1},{2,6},{6,10},{... | collective-permute-start | bytes 36872 | tf_op jit(solution)/shard_map/ppermute | solution.py:13
  42.5 5.9 %collective-permute-start.7 = (f32[3,32,2]{2,1,0:T(8,128)S(1)}, f32[3,32,2]{2,1,0:T(8,128)S(1)}, u32[]{:S(2)}, u32[]{:S(2)}) collective-permute-start(f32[3,32,2]{2,1,0:T(8,128)S(1)} %get-tuple-element.87), channel_id=1, source_target_pairs={{0,4},{4,8},{8,12},{12,0},{1,5},{5,9},{9,13},{13,1},{2,6},{6,10},{... | collective-permute-start | bytes 2312 | tf_op jit(solution)/shard_map/ppermute | solution.py:22
  42.6 5.9 %collective-permute-start.8 = (f32[3,32,2]{2,1,0:T(8,128)S(1)}, f32[3,32,2]{2,1,0:T(8,128)S(1)}, u32[]{:S(2)}, u32[]{:S(2)}) collective-permute-start(f32[3,32,2]{2,1,0:T(8,128)S(1)} %get-tuple-element.88), channel_id=1, source_target_pairs={{4,0},{8,4},{12,8},{0,12},{5,1},{9,5},{13,9},{1,13},{6,2},{10,6},{... | collective-permute-start | bytes 2312 | tf_op jit(solution)/shard_map/ppermute | solution.py:25
  49.1 1.4 %collective-permute-start.10 = (f32[3,2,260]{2,1,0:T(2,128)S(1)}, f32[3,2,260]{2,1,0:T(2,128)S(1)}, u32[]{:S(2)}, u32[]{:S(2)}) collective-permute-start(f32[3,2,260]{2,1,0:T(2,128)S(1)} %get-tuple-element.39), channel_id=1, source_target_pairs={{1,0},{2,1},{3,2},{0,3},{5,4},{6,5},{7,6},{4,7},{9,8},{10,9},{11,1... | collective-permute-start | bytes 18728 | tf_op jit(solution)/shard_map/ppermute | solution.py:25
  49.2 3.1 %collective-permute-start.9 = (f32[3,2,260]{2,1,0:T(2,128)S(1)}, f32[3,2,260]{2,1,0:T(2,128)S(1)}, u32[]{:S(2)}, u32[]{:S(2)}) collective-permute-start(f32[3,2,260]{2,1,0:T(2,128)S(1)} %get-tuple-element.38), channel_id=1, source_target_pairs={{0,1},{1,2},{2,3},{3,0},{4,5},{5,6},{6,7},{7,4},{8,9},{9,10},{10,1... | collective-permute-start | bytes 18728 | tf_op jit(solution)/shard_map/ppermute | solution.py:22
  52.4 5.6 %collective-permute-start.11 = (f32[2,3,2,256]{3,2,1,0:T(2,128)S(1)}, f32[2,3,2,256]{3,2,1,0:T(2,128)S(1)}, u32[]{:S(2)}, u32[]{:S(2)}) collective-permute-start(f32[2,3,2,256]{3,2,1,0:T(2,128)S(1)} %pad_maximum_fusion.11), channel_id=1, source_target_pairs={{0,4},{4,8},{8,12},{12,0},{1,5},{5,9},{9,13},{13,1},{2,6},{6,10},{... | collective-permute-start | bytes 36872 | tf_op jit(solution)/shard_map/ppermute | solution.py:13
  58.0 4.6 %collective-permute-start.12 = (f32[2,3,2,256]{3,2,1,0:T(2,128)S(1)}, f32[2,3,2,256]{3,2,1,0:T(2,128)S(1)}, u32[]{:S(2)}, u32[]{:S(2)}) collective-permute-start(f32[2,3,2,256]{3,2,1,0:T(2,128)S(1)} %broadcast_select_fusion.2), channel_id=1, source_target_pairs={{0,8},{4,12},{8,0},{12,4},{1,9},{5,13},{9,1},{13,5},{2,10},{6,14},... | collective-permute-start | bytes 36872 | tf_op jit(solution)/shard_map/ppermute | solution.py:13
  62.7 5.5 %collective-permute-start.13 = (f32[2,3,2,256]{3,2,1,0:T(2,128)S(1)}, f32[2,3,2,256]{3,2,1,0:T(2,128)S(1)}, u32[]{:S(2)}, u32[]{:S(2)}) collective-permute-start(f32[2,3,2,256]{3,2,1,0:T(2,128)S(1)} %broadcast_select_fusion.3), channel_id=1, source_target_pairs={{0,4},{4,8},{8,12},{12,0},{1,5},{5,9},{9,13},{13,1},{2,6},{6,10},{... | collective-permute-start | bytes 36872 | tf_op jit(solution)/shard_map/ppermute | solution.py:13
  69.7 6.6 %collective-permute-start.14 = (f32[3,32,256]{2,1,0:T(8,128)S(1)}, f32[3,32,256]{2,1,0:T(8,128)S(1)}, u32[]{:S(2)}, u32[]{:S(2)}) collective-permute-start(f32[3,32,256]{2,1,0:T(8,128)S(1)} %fusion.29), channel_id=1, source_target_pairs={{0,4},{4,8},{8,12},{12,0},{1,5},{5,9},{9,13},{13,1},{2,6},{6,10},{... | collective-permute-start | bytes 294920 | tf_op jit(solution)/shard_map/ppermute | solution.py:13
  76.3 6.6 %collective-permute-start.15 = (f32[3,32,256]{2,1,0:T(8,128)S(1)}, f32[3,32,256]{2,1,0:T(8,128)S(1)}, u32[]{:S(2)}, u32[]{:S(2)}) collective-permute-start(f32[3,32,256]{2,1,0:T(8,128)S(1)} %broadcast_select_fusion), channel_id=1, source_target_pairs={{0,8},{4,12},{8,0},{12,4},{1,9},{5,13},{9,1},{13,5},{2,10},{6,14},... | collective-permute-start | bytes 294920 | tf_op jit(solution)/shard_map/ppermute | solution.py:13
  82.9 0.7 copy-start.4
  83.0 6.4 %collective-permute-start.16 = (f32[3,32,256]{2,1,0:T(8,128)S(1)}, f32[3,32,256]{2,1,0:T(8,128)S(1)}, u32[]{:S(2)}, u32[]{:S(2)}) collective-permute-start(f32[3,32,256]{2,1,0:T(8,128)S(1)} %broadcast_select_fusion.1), channel_id=1, source_target_pairs={{0,4},{4,8},{8,12},{12,0},{1,5},{5,9},{9,13},{13,1},{2,6},{6,10},{... | collective-permute-start | bytes 294920 | tf_op jit(solution)/shard_map/ppermute | solution.py:13
where the time goes:
time: 93.1 us; the launch traced here: 92.7 us
  waiting for transfers between devices  56.9 us (61%)
  starting transfers between devices  10.8 us (12%)
  between operations  9.93 us (11%)
  other arithmetic  8.27 us (9%)
  local copies, waits for them, and re-layouts  6.75 us (7%)
    ppermute x9, waiting for transfers between devices, passed_along(): return lax.ppermute(value, axis, pairs)  49.5 us
    ppermute x4, starting transfers between devices, padded_2(): lax.ppermute(lax.slice_in_dim(block, 0, width, axis=dim), axis, backward)  6.67 us
    ppermute x4, waiting for transfers between devices, padded_2(): lax.ppermute(lax.slice_in_dim(block, block.shape[dim] - width, None, axis...  5.39 us
    ppermute x4, starting transfers between devices, padded_2(): lax.ppermute(lax.slice_in_dim(block, block.shape[dim] - width, None, axis...  3.58 us
    ppermute x4, waiting for transfers between devices, padded_2(): lax.ppermute(lax.slice_in_dim(block, 0, width, axis=dim), axis, backward)  2.07 us
    unnamed x12, local copies, waits for them, and re-layouts  1.88 us
  transfers between devices with their start and end apart: 17, of which 14 were waited for; matrix products, arithmetic and copies ran while one was open for 5% of the time, Pallas kernels for 0%

commit v1 on v0

--- a/solution.py
+++ b/solution.py
@@ -1,10 +1,238 @@
+import functools
+
 import jax
 import jax.numpy as jnp
 from jax import lax
+from jax.experimental import pallas as pl
+from jax.experimental.pallas import tpu as pltpu
 from jax.sharding import PartitionSpec as P
 
-time_step = 0.12
-sound_speed = 1.0
+TIME_STEP = 0.12
+SOUND_SPEED = 1.0
+LANES = 128
+HALO = 4
+UNROLL = 8
+
+
+def turned(value, whole, part, lane):
+    lanes = pltpu.roll(value, part, 1)
+    same = pltpu.roll(lanes, whole, 0)
+    before = pltpu.roll(same, 1, 0)
+    return jnp.where(lane < part, before, same)
+
+
+def previous(value, lane):
+    lanes = pltpu.roll(value, 1, 1)
+    return jnp.where(lane == 0, pltpu.roll(lanes, 1, 0), lanes)
+
+
+def following(value, lane):
+    lanes = pltpu.roll(value, LANES - 1, 1)
+    return jnp.where(lane == LANES - 1, pltpu.roll(lanes, value.shape[0] - 1, 0), lanes)
+
+
+def minmod(first, second):
+    return jnp.maximum(jnp.minimum(second, 0.0), jnp.minimum(first, jnp.maximum(second, 0.0)))
+
+
+def sums(left, right):
+    signal = jnp.maximum(jnp.abs(left[1]), jnp.abs(right[1])) + 1.0
+    lower = left[0] * (left[1] + signal)
+    upper = right[0] * (right[1] - signal)
+    return (
+        lower + upper,
+        (left[1] * lower + left[0]) + (right[1] * upper + right[0]),
+        left[2] * lower + right[2] * upper,
+    )
+
+
+def minus(first, second):
+    return tuple(a - b for a, b in zip(first, second))
+
+
+def plus(first, second):
+    return tuple(a + b for a, b in zip(first, second))
+
+
+def primitives(state):
+    inverse = 1.0 / state[0]
+    whole = (state[0], state[1] * inverse, state[2] * inverse)
+    return whole, tuple(0.5 * w for w in whole)
+
+
+def azimuthal(whole, half, lane):
+    normal = (whole[0], whole[2], whole[1])
+    halves = (half[0], half[2], half[1])
+    ahead = minus(tuple(following(h, lane) for h in halves), halves)
+    behind = tuple(previous(a, lane) for a in ahead)
+    slope = tuple(minmod(b, a) for b, a in zip(behind, ahead))
+    left = plus(normal, slope)
+    right = tuple(following(r, lane) for r in minus(normal, slope))
+    face = sums(left, right)
+    out = minus(face, tuple(previous(f, lane) for f in face))
+    return out[0], out[2], out[1]
+
+
+def sweep(load, emit, count, lane, unroll):
+    def advance(row, carry):
+        state = load(row)
+        whole, half = primitives(state)
+        ahead = minus(half, carry["half"])
+        slope = tuple(minmod(b, a) for b, a in zip(carry["ahead"], ahead))
+        right = minus(carry["whole"], slope)
+        left = plus(carry["whole"], slope)
+        face = sums(carry["left"], right)
+        new = {
+            "half": half,
+            "whole": whole,
+            "ahead": ahead,
+            "left": left,
+            "face": face,
+            "turn": azimuthal(carry["whole"], carry["half"], lane),
+        }
+        return new, minus(face, carry["face"])
+
+    def opened(row):
+        first, second, third, fourth = (primitives(load(row + k)) for k in range(4))
+        ahead = [minus(second[1], first[1]), minus(third[1], second[1]), minus(fourth[1], third[1])]
+        slopes = [
+            tuple(minmod(b, a) for b, a in zip(ahead[k], ahead[k + 1])) for k in range(2)
+        ]
+        return {
+            "half": fourth[1],
+            "whole": fourth[0],
+            "ahead": ahead[2],
+            "left": plus(third[0], slopes[1]),
+            "face": sums(plus(second[0], slopes[0]), minus(third[0], slopes[1])),
+            "turn": azimuthal(third[0], third[1], lane),
+        }
+
+    def body(block, carry):
+        for step in range(unroll):
+            row = block * unroll + step
+            new, across = advance(row + 4, carry)
+            emit(row + 2, tuple(a + b for a, b in zip(across, carry["turn"])))
+            carry = new
+        return carry
+
+    opening = opened(0)
+    if count == unroll:
+        body(0, opening)
+    else:
+        lax.fori_loop(0, count // unroll, body, opening)
+
+
+def step_kernel(sizes, *refs):
+    tiles, radials, rows, columns, sub = sizes
+    per_tile = columns // LANES
+    shear_shift, shear_frac, advect_shift, advect_frac, rotation, density, momentum = refs[:7]
+    pieces = refs[7 : 7 + 2 * (tiles - 1)]
+    low, high, density_out, momentum_out, start, middle, remapped = refs[7 + 2 * (tiles - 1) :]
+    lane = lax.broadcasted_iota(jnp.int32, (sub, LANES), 1)
+    az = lax.axis_index("az")
+    radial = lax.axis_index("rad")
+    unroll = UNROLL
+    main = 6
+    end = main + rows + 4
+
+    def place(value, component, row, tile, part):
+        first = row * sub + tile * per_tile + part
+        start[component, pl.ds(first, value.shape[0], stride=sub), :] = value
+
+    for away in range(tiles):
+        tile = az ^ away
+        dens, mom = (density, momentum) if away == 0 else pieces[2 * away - 2 : 2 * away]
+        for part in range(per_tile):
+            cut = slice(part * LANES, (part + 1) * LANES)
+            for row in range(0, rows, 8):
+                place(dens[row : row + 8, cut], 0, main + 2 + row, tile, part)
+                for way in range(2):
+                    place(mom[way, row : row + 8, cut], 1 + way, main + 2 + row, tile, part)
+            for component in range(3):
+                place(low[component, HALO * away : HALO * away + HALO, cut], component, 0, tile, part)
+                place(high[component, HALO * away : HALO * away + HALO, cut], component, end + 2, tile, part)
+
+    def row_of(ref, component, row):
+        return ref[component, pl.ds(pl.multiple_of(row * sub, 8), sub), :]
+
+    def state_of(ref, row):
+        return tuple(row_of(ref, component, row) for component in range(3))
+
+    def put(ref, row, state):
+        for component in range(3):
+            ref[component, pl.ds(pl.multiple_of(row * sub, 8), sub), :] = state[component]
+
+    at_low = radial == 0
+    at_high = radial == radials - 1
+    total = sub * LANES
+
+    def from_below(state, section, here):
+        shift = jnp.where(here, shear_shift[section], 0)
+        weight = jnp.where(here, shear_frac[section], 0.0)
+        moved = tuple(turned(s, shift // LANES, shift % LANES, lane) for s in state)
+        return tuple((1.0 - weight) * m + weight * previous(m, lane) for m in moved)
+
+    def from_above(state, section, here):
+        shift = jnp.where(here, (total - shear_shift[section]) % total, 0)
+        weight = jnp.where(here, shear_frac[section], 0.0)
+        moved = tuple(turned(s, shift // LANES, shift % LANES, lane) for s in state)
+        return tuple((1.0 - weight) * m + weight * following(m, lane) for m in moved)
+
+    for k in range(2):
+        put(start, main + k, from_below(state_of(start, 2 + k), 0, at_low))
+        put(start, end - 2 + k, from_above(state_of(start, end + 2 + k), 0, at_high))
+        put(start, 4 + k, from_above(state_of(start, main + 2 + k), 0, at_low))
+        put(start, end + k, from_below(state_of(start, end - 4 + k), 0, at_high))
+
+    spin = rotation[0]
+
+    def changed(state, double):
+        half_step = 0.5 * TIME_STEP
+        return (
+            state[0] - half_step * double[0],
+            state[1] - half_step * double[1] + (2.0 * TIME_STEP) * spin * state[2],
+            state[2] - half_step * double[2] - (0.5 * TIME_STEP) * spin * state[1],
+        )
+
+    def emit_first(offset, target):
+        def emit(row, double):
+            put(middle, row + target, changed(state_of(start, row + offset), double))
+        return emit
+
+    sweep(lambda row: state_of(start, row + main), emit_first(main, 0), rows, lane, unroll)
+
+    def edge(which, carry):
+        offset = which * end
+        target = which * (rows + 2) - 2
+        sweep(lambda row: state_of(start, row + offset), emit_first(offset, target), 2, lane, 2)
+        return carry
+
+    lax.fori_loop(0, 2, edge, 0)
+    for k in range(2):
+        put(middle, k, from_below(state_of(middle, k), 1, at_low))
+        put(middle, rows + 2 + k, from_above(state_of(middle, rows + 2 + k), 1, at_high))
+
+    def emit_second(row, double):
+        new = changed(state_of(middle, row), double)
+        old = state_of(start, row + main)
+        final = tuple(0.5 * o + 0.5 * n for o, n in zip(old, new))
+        shift = advect_shift[row - 2]
+        weight = advect_frac[row - 2]
+        moved = tuple(turned(f, shift // LANES, shift % LANES, lane) for f in final)
+        put(remapped, row - 2, tuple((1.0 - weight) * m + weight * previous(m, lane) for m in moved))
+
+    sweep(lambda row: state_of(middle, row), emit_second, rows, lane, unroll)
+
+    for part in range(per_tile):
+        cut = slice(part * LANES, (part + 1) * LANES)
+        for row in range(0, rows, 8):
+            first = row * sub + az * per_tile + part
+            for component in range(3):
+                value = remapped[component, pl.ds(first, 8, stride=sub), :]
+                if component == 0:
+                    density_out[row : row + 8, cut] = value
+                else:
+                    momentum_out[component - 1, row : row + 8, cut] = value
 
 
 def passed_along(value, axis, steps):
@@ -27,7 +255,7 @@
     return block
 
 
-def minmod(first, second):
+def signed_minmod(first, second):
     return 0.5 * (jnp.sign(first) + jnp.sign(second)) * jnp.minimum(jnp.abs(first), jnp.abs(second))
 
 
@@ -40,7 +268,7 @@
     fluxes = jnp.stack(
         [
             mass_flux,
-            mass_flux * state[1] + sound_speed * sound_speed * state[0],
+            mass_flux * state[1] + SOUND_SPEED * SOUND_SPEED * state[0],
             mass_flux * state[2],
         ]
     )
@@ -51,7 +279,7 @@
 def face_flux(left_state, right_state):
     left_flux, left_cons = physical(left_state)
     right_flux, right_cons = physical(right_state)
-    signal = jnp.maximum(jnp.abs(left_state[1]), jnp.abs(right_state[1])) + sound_speed
+    signal = jnp.maximum(jnp.abs(left_state[1]), jnp.abs(right_state[1])) + SOUND_SPEED
     return 0.5 * (left_flux + right_flux) - 0.5 * signal * (right_cons - left_cons)
 
 
@@ -62,7 +290,7 @@
 
 
 def sweep_axis(prims, direction):
-    slopes = minmod(
+    slopes = signed_minmod(
         trimmed(prims, 1, 1, direction) - trimmed(prims, 0, 2, direction),
         trimmed(prims, 2, 0, direction) - trimmed(prims, 1, 1, direction),
     )
@@ -145,14 +373,68 @@
     return (1.0 - weight) * aligned[:, :, 1 : tile_width + 1] + weight * aligned[:, :, :tile_width]
 
 
-def per_device(density, momentum, shear_shift, shear_frac, advect_shift, advect_frac, rotation):
+def wide_ring(density, momentum, shear_shift, shear_frac, advect_shift, advect_frac, rotation):
     state = jnp.concatenate([density[None], momentum], axis=0)
-    middle = state + time_step * tendency(state, shear_shift[0], shear_frac[0], rotation[0])
+    middle = state + TIME_STEP * tendency(state, shear_shift[0], shear_frac[0], rotation[0])
     final = 0.5 * state + 0.5 * (
-        middle + time_step * tendency(middle, shear_shift[1], shear_frac[1], rotation[0])
+        middle + TIME_STEP * tendency(middle, shear_shift[1], shear_frac[1], rotation[0])
     )
     remapped = remap_rows(final, advect_shift, advect_frac)
     return (remapped[0], remapped[1:])
+
+
+def near(value):
+    return pltpu.with_memory_space_constraint(value, pltpu.VMEM)
+
+
+def per_device(density, momentum, shear_shift, shear_frac, advect_shift, advect_frac, rotation):
+    tiles = lax.axis_size("az")
+    radials = lax.axis_size("rad")
+    rows, columns = density.shape
+    sub = tiles * columns // LANES
+    if sub != 8 or rows % 8:
+        return wide_ring(
+            density, momentum, shear_shift, shear_frac, advect_shift, advect_frac, rotation
+        )
+
+    def across(value, away):
+        return lax.ppermute(value, "az", [(i, i ^ away) for i in range(tiles)])
+
+    def along(value, steps):
+        return lax.ppermute(value, "rad", [(i, (i + steps) % radials) for i in range(radials)])
+
+    pieces = []
+    for away in range(1, tiles):
+        pieces += [across(density, away), across(momentum, away)]
+
+    def edge(cut):
+        parts = [density[None, cut], momentum[:, cut]]
+        blocks = [jnp.concatenate(parts, axis=0)]
+        for away in range(1, tiles):
+            blocks.append(jnp.concatenate([pieces[2 * away - 2][None, cut], pieces[2 * away - 1][:, cut]], axis=0))
+        return jnp.concatenate(blocks, axis=1)
+
+    low = along(edge(slice(rows - HALO, rows)), 1)
+    high = along(edge(slice(0, HALO)), -1)
+
+    vmem = pl.BlockSpec(memory_space=pltpu.VMEM)
+    smem = pl.BlockSpec(memory_space=pltpu.SMEM)
+    operands = [near(p) for p in pieces] + [near(low), near(high)]
+    return pl.pallas_call(
+        functools.partial(step_kernel, (tiles, radials, rows, columns, sub)),
+        out_shape=[
+            jax.ShapeDtypeStruct(density.shape, density.dtype),
+            jax.ShapeDtypeStruct(momentum.shape, momentum.dtype),
+        ],
+        in_specs=[smem] * 5 + [vmem] * (2 + len(operands)),
+        out_specs=[vmem, vmem],
+        scratch_shapes=[
+            pltpu.VMEM((3, (rows + 16) * sub, LANES), jnp.float32),
+            pltpu.VMEM((3, (rows + 4) * sub, LANES), jnp.float32),
+            pltpu.VMEM((3, rows * sub, LANES), jnp.float32),
+        ],
+        compiler_params=pltpu.CompilerParams(vmem_limit_bytes=40 * 2**20),
+    )(shear_shift, shear_frac, advect_shift, advect_frac, rotation, density, momentum, *operands)
 
 
 def solution(mesh):

time: 93.1 us -> 27.4 us (0.29)
  the two profiles are of different devices: /device:TPU:0 before, /device:TPU:1 now
where the time goes in v1:
time: 27.4 us; the launch traced here: 27.2 us
  starting transfers between devices  11 us (40%)
  waiting for transfers between devices  7.97 us (29%)
  Pallas kernels  5.95 us (22%)
  between operations  1.4 us (5%)
  local copies, waits for them, and re-layouts  0.86 us (3%)
    ppermute x6, starting transfers between devices, across(): return lax.ppermute(value, 'az', [(i, i ^ away) for i in range(tiles)])  8.16 us
    pallas_call x1, Pallas kernels, per_device(): pl.pallas_call(functools.partial(step_kernel, (tiles, radials, rows, colu...  5.95 us
    ppermute x6, waiting for transfers between devices, across(): return lax.ppermute(value, 'az', [(i, i ^ away) for i in range(tiles)])  5.12 us
    ppermute x2, starting transfers between devices, along(): lax.ppermute(value, 'rad', [(i, (i + steps) % radials) for i in range(rad...  2.87 us
    ppermute x2, waiting for transfers between devices, along(): lax.ppermute(value, 'rad', [(i, (i + steps) % radials) for i in range(rad...  2.85 us
    slice x1, local copies, waits for them, and re-layouts, edge(): parts = [density[None, cut], momentum[:, cut]]  0.79 us
  transfers between devices with their start and end apart: 8, of which 4 were waited for; matrix products, arithmetic and copies ran while one was open for 3% of the time, Pallas kernels for 0%

profile of v1, /device:TPU:1, one launch (start us, length us, event | category | flops | bytes accessed | tf_op | source)
XLA Modules:
  0.0 27.2 jit_solution(5940493885546472274)
XLA Ops:
  0.6 0.0 copy-start.1
  0.6 4.2 %collective-permute-start.4 = (f32[32,256]{1,0:T(8,128)}, f32[32,256]{1,0:T(8,128)S(1)}, u32[]{:S(2)}, u32[]{:S(2)}) collective-permute-start(f32[32,256]{1,0:T(8,128)} %refs_5_.1), channel_id=1, source_target_pairs={{0,12},{4,8},{8,4},{12,0},{1,13},{5,9},{9,5},{13,1},{2,14},{6,10},... | collective-permute-start | bytes 98312 | tf_op jit(solution)/shard_map/ppermute | solution.py:401
  4.9 0.0 collective-permute-start.2
  4.9 0.4 %collective-permute-start = (f32[32,256]{1,0:T(8,128)}, f32[32,256]{1,0:T(8,128)S(1)}, u32[]{:S(2)}, u32[]{:S(2)}) collective-permute-start(f32[32,256]{1,0:T(8,128)} %refs_5_.1), channel_id=1, source_target_pairs={{0,4},{4,0},{8,12},{12,8},{1,5},{5,1},{9,13},{13,9},{2,6},{6,2},{1... | collective-permute-start | bytes 98312 | tf_op jit(solution)/shard_map/ppermute | solution.py:401
  5.2 3.2 %collective-permute-start.5 = (f32[2,32,256]{2,1,0:T(8,128)}, f32[2,32,256]{2,1,0:T(8,128)S(1)}, u32[]{:S(2)}, u32[]{:S(2)}) collective-permute-start(f32[2,32,256]{2,1,0:T(8,128)} %refs_6_.1), channel_id=1, source_target_pairs={{0,12},{4,8},{8,4},{12,0},{1,13},{5,9},{9,5},{13,1},{2,14},{6,10},... | collective-permute-start | bytes 196616 | tf_op jit(solution)/shard_map/ppermute | solution.py:401
  8.4 0.0 collective-permute-start.3
  8.4 0.8 %fusion = (f32[2,4,256]{2,1,0:T(4,128)S(1)}, f32[2,4,256]{2,1,0:T(4,128)S(1)}) fusion(f32[2,32,256]{2,1,0:T(8,128)} %refs_6_.1), kind=kLoop, calls=%fused_computation.10 | loop fusion | bytes 32768 | tf_op jit(solution)/shard_map/slice | solution.py:411
  9.2 0.0 copy-done.1
  9.2 0.0 collective-permute-done.4.refs_11_
  9.2 0.4 %collective-permute-start.1 = (f32[2,32,256]{2,1,0:T(8,128)}, f32[2,32,256]{2,1,0:T(8,128)S(1)}, u32[]{:S(2)}, u32[]{:S(2)}) collective-permute-start(f32[2,32,256]{2,1,0:T(8,128)} %refs_6_.1), channel_id=1, source_target_pairs={{0,4},{4,0},{8,12},{12,8},{1,5},{5,1},{9,13},{13,9},{2,6},{6,2},{1... | collective-permute-start | bytes 196616 | tf_op jit(solution)/shard_map/ppermute | solution.py:401
  9.6 0.0 collective-permute-done.2.refs_9_
  9.6 0.0 collective-permute-done.refs_7_
  9.6 1.1 %collective-permute-done.5.refs_12_ = f32[2,32,256]{2,1,0:T(8,128)S(1)} collective-permute-done((f32[2,32,256]{2,1,0:T(8,128)}, f32[2,32,256]{2,1,0:T(8,128)S(1)}, u32[]{:S(2)}, u32[]{:S(2)}) %collective-permute-start.5) | collective-permute-done | bytes 65568 | tf_op jit(solution)/shard_map/ppermute | solution.py:401
  10.7 4.0 %collective-permute-done.3.refs_10_ = f32[2,32,256]{2,1,0:T(8,128)S(1)} collective-permute-done((f32[2,32,256]{2,1,0:T(8,128)}, f32[2,32,256]{2,1,0:T(8,128)S(1)}, u32[]{:S(2)}, u32[]{:S(2)}) %collective-permute-start.3) | collective-permute-done | bytes 65568 | tf_op jit(solution)/shard_map/ppermute | solution.py:401
  14.8 0.0 collective-permute-done.1.refs_8_
  14.8 0.0 copy-start
  14.8 2.8 %collective-permute-start.6 = (f32[3,16,256]{2,1,0:T(8,128)S(1)}, f32[3,16,256]{2,1,0:T(8,128)S(1)}, u32[]{:S(2)}, u32[]{:S(2)}) collective-permute-start(f32[3,16,256]{2,1,0:T(8,128)S(1)} %maximum_maximum_fusion), channel_id=1, source_target_pairs={{0,1},{1,2},{2,3},{3,0},{4,5},{5,6},{6,7},{7,4},{8,9},{9,10},{10,1... | collective-permute-start | bytes 147464 | tf_op jit(solution)/shard_map/ppermute | solution.py:404
  17.6 0.0 copy-start.5
  17.7 0.0 copy-start.2
  17.7 0.0 copy-start.3
  17.7 0.0 copy-start.4
  17.7 0.1 collective-permute-start.7
  18.4 0.4 %collective-permute-done.6.refs_13_ = f32[3,16,256]{2,1,0:T(8,128)S(1)} collective-permute-done((f32[3,16,256]{2,1,0:T(8,128)S(1)}, f32[3,16,256]{2,1,0:T(8,128)S(1)}, u32[]{:S(2)}, u32[]{:S(2)}) %collective-permute-start.6) | collective-permute-done | bytes 49184 | tf_op jit(solution)/shard_map/ppermute | solution.py:404
  18.8 2.4 %collective-permute-done.7.refs_14_ = f32[3,16,256]{2,1,0:T(8,128)S(1)} collective-permute-done((f32[3,16,256]{2,1,0:T(8,128)S(1)}, f32[3,16,256]{2,1,0:T(8,128)S(1)}, u32[]{:S(2)}, u32[]{:S(2)}) %collective-permute-start.7) | collective-permute-done | bytes 49184 | tf_op jit(solution)/shard_map/ppermute | solution.py:404
  21.3 0.0 copy-done
  21.3 0.0 copy-done.5
  21.3 0.0 copy-done.2
  21.3 0.0 copy-done.3
  21.3 0.0 copy-done.4
  21.3 5.9 %shard_map.86 = (f32[32,256]{1,0:T(8,128)}, f32[2,32,256]{2,1,0:T(8,128)}) custom-call(s32[2]{0:T(128)S(1)} %copy-done.2, f32[2]{0:T(128)S(1)} %copy-done.3, s32[32]{0:T(128)S(1)} %copy-done.4, f32[32]{0:T(128)S(1)} %copy-done.5, f32[1]{0:T(128)S(6)} %copy.9.refs_4_, f32[32,256]{1,0:T(8,128)S(1)} %copy-done.1, f32[2,32,256]{2,1,0:T(8,128)S(1)} %copy-done, ...), custom_call_target="tpu_custom_call" | custom-call | tf_op jit(solution)/shard_map/pallas_call | solution.py:423
  (9 shorter events, 0.1 us)
Async XLA Ops:
  0.6 8.6 %copy-start.1 = (f32[32,256]{1,0:T(8,128)S(1)}, f32[32,256]{1,0:T(8,128)}, u32[]{:S(2)}) copy-start(f32[32,256]{1,0:T(8,128)} %refs_5_.1) | copy-start | bytes 98308
  0.6 8.6 %collective-permute-start.4 = (f32[32,256]{1,0:T(8,128)}, f32[32,256]{1,0:T(8,128)S(1)}, u32[]{:S(2)}, u32[]{:S(2)}) collective-permute-start(f32[32,256]{1,0:T(8,128)} %refs_5_.1), channel_id=1, source_target_pairs={{0,12},{4,8},{8,4},{12,0},{1,13},{5,9},{9,5},{13,1},{2,14},{6,10},... | collective-permute-start | bytes 98312 | tf_op jit(solution)/shard_map/ppermute | solution.py:401
  4.9 4.8 %collective-permute-start.2 = (f32[32,256]{1,0:T(8,128)}, f32[32,256]{1,0:T(8,128)S(1)}, u32[]{:S(2)}, u32[]{:S(2)}) collective-permute-start(f32[32,256]{1,0:T(8,128)} %refs_5_.1), channel_id=1, source_target_pairs={{0,8},{4,12},{8,0},{12,4},{1,9},{5,13},{9,1},{13,5},{2,10},{6,14},... | collective-permute-start | bytes 98312 | tf_op jit(solution)/shard_map/ppermute | solution.py:401
  4.9 4.8 %collective-permute-start = (f32[32,256]{1,0:T(8,128)}, f32[32,256]{1,0:T(8,128)S(1)}, u32[]{:S(2)}, u32[]{:S(2)}) collective-permute-start(f32[32,256]{1,0:T(8,128)} %refs_5_.1), channel_id=1, source_target_pairs={{0,4},{4,0},{8,12},{12,8},{1,5},{5,1},{9,13},{13,9},{2,6},{6,2},{1... | collective-permute-start | bytes 98312 | tf_op jit(solution)/shard_map/ppermute | solution.py:401
  5.2 5.5 %collective-permute-start.5 = (f32[2,32,256]{2,1,0:T(8,128)}, f32[2,32,256]{2,1,0:T(8,128)S(1)}, u32[]{:S(2)}, u32[]{:S(2)}) collective-permute-start(f32[2,32,256]{2,1,0:T(8,128)} %refs_6_.1), channel_id=1, source_target_pairs={{0,12},{4,8},{8,4},{12,0},{1,13},{5,9},{9,5},{13,1},{2,14},{6,10},... | collective-permute-start | bytes 196616 | tf_op jit(solution)/shard_map/ppermute | solution.py:401
  8.4 6.4 %collective-permute-start.3 = (f32[2,32,256]{2,1,0:T(8,128)}, f32[2,32,256]{2,1,0:T(8,128)S(1)}, u32[]{:S(2)}, u32[]{:S(2)}) collective-permute-start(f32[2,32,256]{2,1,0:T(8,128)} %refs_6_.1), channel_id=1, source_target_pairs={{0,8},{4,12},{8,0},{12,4},{1,9},{5,13},{9,1},{13,5},{2,10},{6,14},... | collective-permute-start | bytes 196616 | tf_op jit(solution)/shard_map/ppermute | solution.py:401
  9.2 5.6 %collective-permute-start.1 = (f32[2,32,256]{2,1,0:T(8,128)}, f32[2,32,256]{2,1,0:T(8,128)S(1)}, u32[]{:S(2)}, u32[]{:S(2)}) collective-permute-start(f32[2,32,256]{2,1,0:T(8,128)} %refs_6_.1), channel_id=1, source_target_pairs={{0,4},{4,0},{8,12},{12,8},{1,5},{5,1},{9,13},{13,9},{2,6},{6,2},{1... | collective-permute-start | bytes 196616 | tf_op jit(solution)/shard_map/ppermute | solution.py:401
  14.8 6.5 %copy-start = (f32[2,32,256]{2,1,0:T(8,128)S(1)}, f32[2,32,256]{2,1,0:T(8,128)}, u32[]{:S(2)}) copy-start(f32[2,32,256]{2,1,0:T(8,128)} %refs_6_.1) | copy-start | bytes 196612
  14.8 4.0 %collective-permute-start.6 = (f32[3,16,256]{2,1,0:T(8,128)S(1)}, f32[3,16,256]{2,1,0:T(8,128)S(1)}, u32[]{:S(2)}, u32[]{:S(2)}) collective-permute-start(f32[3,16,256]{2,1,0:T(8,128)S(1)} %maximum_maximum_fusion), channel_id=1, source_target_pairs={{0,1},{1,2},{2,3},{3,0},{4,5},{5,6},{6,7},{7,4},{8,9},{9,10},{10,1... | collective-permute-start | bytes 147464 | tf_op jit(solution)/shard_map/ppermute | solution.py:404
  17.6 3.6 %copy-start.5 = (f32[32]{0:T(128)S(1)}, f32[32]{0:T(128)}, u32[]{:S(2)}) copy-start(f32[32]{0:T(128)} %refs_3_.1) | copy-start | bytes 388
  17.7 3.6 %copy-start.2 = (s32[2]{0:T(128)S(1)}, s32[2]{0:T(128)}, u32[]{:S(2)}) copy-start(s32[2]{0:T(128)} %refs_0_.1) | copy-start | bytes 28
  17.7 3.6 %copy-start.3 = (f32[2]{0:T(128)S(1)}, f32[2]{0:T(128)}, u32[]{:S(2)}) copy-start(f32[2]{0:T(128)} %refs_1_.1) | copy-start | bytes 28
  17.7 3.6 %copy-start.4 = (s32[32]{0:T(128)S(1)}, s32[32]{0:T(128)}, u32[]{:S(2)}) copy-start(s32[32]{0:T(128)} %refs_2_.1) | copy-start | bytes 388
  17.7 3.6 %collective-permute-start.7 = (f32[3,16,256]{2,1,0:T(8,128)S(1)}, f32[3,16,256]{2,1,0:T(8,128)S(1)}, u32[]{:S(2)}, u32[]{:S(2)}) collective-permute-start(f32[3,16,256]{2,1,0:T(8,128)S(1)} %maximum_maximum_fusion.1), channel_id=1, source_target_pairs={{0,3},{1,0},{2,1},{3,2},{4,7},{5,4},{6,5},{7,6},{8,11},{9,8},{10,9... | collective-permute-start | bytes 147464 | tf_op jit(solution)/shard_map/ppermute | solution.py:404

commit v2 on v1

--- a/solution.py
+++ b/solution.py
@@ -11,7 +11,9 @@
 SOUND_SPEED = 1.0
 LANES = 128
 HALO = 4
-UNROLL = 8
+EDGE_ORDER = (1, 3, 2)
+INNER_ORDER = (2, 1, 3)
+LOOPS = (1, 1, 2)
 
 
 def turned(value, whole, part, lane):
@@ -56,84 +58,92 @@
 
 def primitives(state):
     inverse = 1.0 / state[0]
-    whole = (state[0], state[1] * inverse, state[2] * inverse)
-    return whole, tuple(0.5 * w for w in whole)
-
-
-def azimuthal(whole, half, lane):
-    normal = (whole[0], whole[2], whole[1])
-    halves = (half[0], half[2], half[1])
-    ahead = minus(tuple(following(h, lane) for h in halves), halves)
-    behind = tuple(previous(a, lane) for a in ahead)
-    slope = tuple(minmod(b, a) for b, a in zip(behind, ahead))
-    left = plus(normal, slope)
-    right = tuple(following(r, lane) for r in minus(normal, slope))
-    face = sums(left, right)
-    out = minus(face, tuple(previous(f, lane) for f in face))
-    return out[0], out[2], out[1]
-
-
-def sweep(load, emit, count, lane, unroll):
+    return state[0], state[1] * inverse, state[2] * inverse
+
+
+def azimuthal(whole):
+    return whole[0], whole[2], whole[1]
+
+
+def repeated(first, count, loops, body):
+    each = count // loops
+
+    def block(turn, carry):
+        for step in range(each):
+            body(first + turn * each + step)
+        return carry
+
+    if loops == 1:
+        block(0, 0)
+    else:
+        lax.fori_loop(0, loops, block, 0)
+
+
+def radial_sweep(load, emit, first, count, loops):
+    def half_steps(above, below):
+        return tuple(0.5 * (a - b) for a, b in zip(above, below))
+
     def advance(row, carry):
-        state = load(row)
-        whole, half = primitives(state)
-        ahead = minus(half, carry["half"])
+        whole = load(row)
+        ahead = half_steps(whole, carry["whole"])
         slope = tuple(minmod(b, a) for b, a in zip(carry["ahead"], ahead))
-        right = minus(carry["whole"], slope)
-        left = plus(carry["whole"], slope)
-        face = sums(carry["left"], right)
-        new = {
-            "half": half,
-            "whole": whole,
-            "ahead": ahead,
-            "left": left,
-            "face": face,
-            "turn": azimuthal(carry["whole"], carry["half"], lane),
-        }
+        face = sums(carry["left"], minus(carry["whole"], slope))
+        new = {"whole": whole, "ahead": ahead, "left": plus(carry["whole"], slope), "face": face}
         return new, minus(face, carry["face"])
 
-    def opened(row):
-        first, second, third, fourth = (primitives(load(row + k)) for k in range(4))
-        ahead = [minus(second[1], first[1]), minus(third[1], second[1]), minus(fourth[1], third[1])]
-        slopes = [
-            tuple(minmod(b, a) for b, a in zip(ahead[k], ahead[k + 1])) for k in range(2)
-        ]
-        return {
-            "half": fourth[1],
-            "whole": fourth[0],
-            "ahead": ahead[2],
-            "left": plus(third[0], slopes[1]),
-            "face": sums(plus(second[0], slopes[0]), minus(third[0], slopes[1])),
-            "turn": azimuthal(third[0], third[1], lane),
-        }
-
-    def body(block, carry):
-        for step in range(unroll):
-            row = block * unroll + step
-            new, across = advance(row + 4, carry)
-            emit(row + 2, tuple(a + b for a, b in zip(across, carry["turn"])))
-            carry = new
+    rows = [load(first - 2 + k) for k in range(4)]
+    ahead = [half_steps(rows[k + 1], rows[k]) for k in range(3)]
+    slopes = [tuple(minmod(b, a) for b, a in zip(ahead[k], ahead[k + 1])) for k in range(2)]
+    carry = {
+        "whole": rows[3],
+        "ahead": ahead[2],
+        "left": plus(rows[2], slopes[1]),
+        "face": sums(plus(rows[1], slopes[0]), minus(rows[2], slopes[1])),
+    }
+    each = count // loops
+
+    def block(turn, carry):
+        for step in range(each):
+            row = first + turn * each + step
+            carry, across = advance(row + 2, carry)
+            emit(row, across)
         return carry
 
-    opening = opened(0)
-    if count == unroll:
-        body(0, opening)
+    if loops == 1:
+        block(0, carry)
     else:
-        lax.fori_loop(0, count // unroll, body, opening)
+        lax.fori_loop(0, loops, block, carry)
+
+
+def split_kernel(*refs):
+    density, momentum, edges, inner = refs[4:8]
+    for given, kept in zip(refs[:4], refs[8:]):
+        for place in range(given.shape[0]):
+            kept[place] = given[place]
+    rows = density.shape[0]
+    for component, take in enumerate(
+        (lambda cut: density[cut, :], lambda cut: momentum[0, cut, :], lambda cut: momentum[1, cut, :])
+    ):
+        edges[component, 0:HALO] = take(slice(0, HALO))
+        edges[component, HALO : 2 * HALO] = take(slice(rows - HALO, rows))
+        inner[component] = take(slice(HALO, rows - HALO))
 
 
 def step_kernel(sizes, *refs):
     tiles, radials, rows, columns, sub = sizes
     per_tile = columns // LANES
-    shear_shift, shear_frac, advect_shift, advect_frac, rotation, density, momentum = refs[:7]
-    pieces = refs[7 : 7 + 2 * (tiles - 1)]
-    low, high, density_out, momentum_out, start, middle, remapped = refs[7 + 2 * (tiles - 1) :]
+    shear_shift, shear_frac, advect_shift, advect_frac, rotation = refs[:5]
+    edges = refs[5 : 5 + tiles]
+    inners = refs[5 + tiles : 5 + 2 * tiles]
+    within, between, density_out, momentum_out, start, middle, remapped, whole, lower, upper, faces = refs[5 + 2 * tiles :]
     lane = lax.broadcasted_iota(jnp.int32, (sub, LANES), 1)
     az = lax.axis_index("az")
     radial = lax.axis_index("rad")
-    unroll = UNROLL
     main = 6
     end = main + rows + 4
+    odd = radial % 2
+    spot_within = jnp.where(odd == 1, 0, end + 2)
+    spot_between = jnp.where(odd == 1, end + 2, 0)
 
     def place(value, component, row, tile, part):
         first = row * sub + tile * per_tile + part
@@ -141,26 +151,26 @@
 
     for away in range(tiles):
         tile = az ^ away
-        dens, mom = (density, momentum) if away == 0 else pieces[2 * away - 2 : 2 * away]
         for part in range(per_tile):
             cut = slice(part * LANES, (part + 1) * LANES)
-            for row in range(0, rows, 8):
-                place(dens[row : row + 8, cut], 0, main + 2 + row, tile, part)
-                for way in range(2):
-                    place(mom[way, row : row + 8, cut], 1 + way, main + 2 + row, tile, part)
             for component in range(3):
-                place(low[component, HALO * away : HALO * away + HALO, cut], component, 0, tile, part)
-                place(high[component, HALO * away : HALO * away + HALO, cut], component, end + 2, tile, part)
+                place(edges[away][component, 0:HALO, cut], component, main + 2, tile, part)
+                place(edges[away][component, HALO : 2 * HALO, cut], component, end - 2 - HALO, tile, part)
+                for row in range(0, rows - 2 * HALO, 8):
+                    place(inners[away][component, row : row + 8, cut], component, main + 2 + HALO + row, tile, part)
+                border = slice(HALO * away, HALO * away + HALO)
+                place(within[component, border, cut], component, spot_within, tile, part)
+                place(between[component, border, cut], component, spot_between, tile, part)
 
     def row_of(ref, component, row):
-        return ref[component, pl.ds(pl.multiple_of(row * sub, 8), sub), :]
+        return ref[component, pl.ds(row * sub if isinstance(row, int) else pl.multiple_of(row * sub, 8), sub), :]
 
     def state_of(ref, row):
         return tuple(row_of(ref, component, row) for component in range(3))
 
     def put(ref, row, state):
         for component in range(3):
-            ref[component, pl.ds(pl.multiple_of(row * sub, 8), sub), :] = state[component]
+            ref[component, pl.ds(row * sub if isinstance(row, int) else pl.multiple_of(row * sub, 8), sub), :] = state[component]
 
     at_low = radial == 0
     at_high = radial == radials - 1
@@ -184,7 +194,7 @@
         put(start, 4 + k, from_above(state_of(start, main + 2 + k), 0, at_low))
         put(start, end + k, from_below(state_of(start, end - 4 + k), 0, at_high))
 
-    spin = rotation[0]
+    spin = rotation[...]
 
     def changed(state, double):
         half_step = 0.5 * TIME_STEP
@@ -194,26 +204,51 @@
             state[2] - half_step * double[2] - (0.5 * TIME_STEP) * spin * state[1],
         )
 
-    def emit_first(offset, target):
-        def emit(row, double):
-            put(middle, row + target, changed(state_of(start, row + offset), double))
+    def slopes(source, row):
+        values = primitives(state_of(source, row))
+        put(whole, row, values)
+        normal = azimuthal(values)
+        halves = tuple(0.5 * n for n in normal)
+        slope = tuple(
+            minmod(h - previous(h, lane), following(h, lane) - h) for h in halves
+        )
+        put(lower, row, plus(normal, slope))
+        put(upper, row, minus(normal, slope))
+
+    def meet(row):
+        right = tuple(following(r, lane) for r in state_of(upper, row))
+        put(faces, row, sums(state_of(lower, row), right))
+
+    def turn(row):
+        face = state_of(faces, row)
+        return azimuthal(minus(face, tuple(previous(f, lane) for f in face)))
+
+    def only(source, row):
+        put(whole, row, primitives(state_of(source, row)))
+
+    def emit_first(shift):
+        def emit(row, across):
+            put(middle, row + shift, changed(state_of(start, row), plus(across, turn(row))))
         return emit
 
-    sweep(lambda row: state_of(start, row + main), emit_first(main, 0), rows, lane, unroll)
-
-    def edge(which, carry):
-        offset = which * end
-        target = which * (rows + 2) - 2
-        sweep(lambda row: state_of(start, row + offset), emit_first(offset, target), 2, lane, 2)
-        return carry
-
-    lax.fori_loop(0, 2, edge, 0)
+    for row in (0, 1, 4, 5, main, main + 1, end - 2, end - 1, end, end + 1, end + 4, end + 5):
+        only(start, row)
+    for row in (2, 3, end + 2, end + 3):
+        slopes(start, row)
+    repeated(main + 2, rows, LOOPS[0], lambda row: slopes(start, row))
+    for row in (2, 3, end + 2, end + 3):
+        meet(row)
+    repeated(main + 2, rows, LOOPS[1], meet)
+    radial_sweep(lambda row: state_of(whole, row), emit_first(-2), 2, 2, 1)
+    radial_sweep(lambda row: state_of(whole, row), emit_first(rows - end), end + 2, 2, 1)
+    radial_sweep(lambda row: state_of(whole, row), emit_first(-main), main + 2, rows, LOOPS[2])
+
     for k in range(2):
         put(middle, k, from_below(state_of(middle, k), 1, at_low))
         put(middle, rows + 2 + k, from_above(state_of(middle, rows + 2 + k), 1, at_high))
 
-    def emit_second(row, double):
-        new = changed(state_of(middle, row), double)
+    def emit_second(row, across):
+        new = changed(state_of(middle, row), plus(across, turn(row)))
         old = state_of(start, row + main)
         final = tuple(0.5 * o + 0.5 * n for o, n in zip(old, new))
         shift = advect_shift[row - 2]
@@ -221,7 +256,11 @@
         moved = tuple(turned(f, shift // LANES, shift % LANES, lane) for f in final)
         put(remapped, row - 2, tuple((1.0 - weight) * m + weight * previous(m, lane) for m in moved))
 
-    sweep(lambda row: state_of(middle, row), emit_second, rows, lane, unroll)
+    for row in (0, 1, rows + 2, rows + 3):
+        only(middle, row)
+    repeated(2, rows, LOOPS[0], lambda row: slopes(middle, row))
+    repeated(2, rows, LOOPS[1], meet)
+    radial_sweep(lambda row: state_of(whole, row), emit_second, 2, rows, LOOPS[2])
 
     for part in range(per_tile):
         cut = slice(part * LANES, (part + 1) * LANES)
@@ -392,49 +431,62 @@
     radials = lax.axis_size("rad")
     rows, columns = density.shape
     sub = tiles * columns // LANES
-    if sub != 8 or rows % 8:
+    if tiles != 4 or sub != 8 or rows % 8 or radials % 2:
         return wide_ring(
             density, momentum, shear_shift, shear_frac, advect_shift, advect_frac, rotation
         )
 
+    vmem = pl.BlockSpec(memory_space=pltpu.VMEM)
+    smem = pl.BlockSpec(memory_space=pltpu.SMEM)
+
     def across(value, away):
         return lax.ppermute(value, "az", [(i, i ^ away) for i in range(tiles)])
 
-    def along(value, steps):
-        return lax.ppermute(value, "rad", [(i, (i + steps) % radials) for i in range(radials)])
-
-    pieces = []
-    for away in range(1, tiles):
-        pieces += [across(density, away), across(momentum, away)]
-
-    def edge(cut):
-        parts = [density[None, cut], momentum[:, cut]]
-        blocks = [jnp.concatenate(parts, axis=0)]
-        for away in range(1, tiles):
-            blocks.append(jnp.concatenate([pieces[2 * away - 2][None, cut], pieces[2 * away - 1][:, cut]], axis=0))
-        return jnp.concatenate(blocks, axis=1)
-
-    low = along(edge(slice(rows - HALO, rows)), 1)
-    high = along(edge(slice(0, HALO)), -1)
-
-    vmem = pl.BlockSpec(memory_space=pltpu.VMEM)
-    smem = pl.BlockSpec(memory_space=pltpu.SMEM)
-    operands = [near(p) for p in pieces] + [near(low), near(high)]
+    def swapped(value, lower):
+        pairs = [((i + lower) % radials, (i + lower + 1) % radials) for i in range(0, radials, 2)]
+        return lax.ppermute(value, "rad", pairs + [(b, a) for a, b in pairs])
+
+    scalars = (shear_shift, shear_frac, advect_shift, advect_frac)
+    spin = jnp.broadcast_to(rotation[:, None], (sub, LANES))
+    edge, inner, *kept = pl.pallas_call(
+        split_kernel,
+        out_shape=[
+            pltpu.VMEM((3, 2 * HALO, columns), jnp.float32),
+            pltpu.VMEM((3, rows - 2 * HALO, columns), jnp.float32),
+        ]
+        + [pltpu.SMEM(s.shape, s.dtype) for s in scalars],
+        in_specs=[smem] * 4 + [vmem] * 2,
+        out_specs=[vmem] * 2 + [smem] * 4,
+    )(*scalars, density, momentum)
+    edges = {0: edge}
+    inners = {0: inner}
+    for away in EDGE_ORDER:
+        edges[away] = across(edge, away)
+    for away in INNER_ORDER:
+        inners[away] = across(inner, away)
+    top = jnp.concatenate([edges[away][:, :HALO] for away in range(tiles)], axis=1)
+    bottom = jnp.concatenate([edges[away][:, HALO:] for away in range(tiles)], axis=1)
+    odd = lax.axis_index("rad") % 2 == 1
+    within = swapped(jnp.where(odd, top, bottom), 0)
+    between = swapped(jnp.where(odd, bottom, top), 1)
+    operands = [edges[away] for away in range(tiles)] + [inners[away] for away in range(tiles)]
+    operands = [near(p) for p in [spin] + operands + [within, between]]
     return pl.pallas_call(
         functools.partial(step_kernel, (tiles, radials, rows, columns, sub)),
         out_shape=[
             jax.ShapeDtypeStruct(density.shape, density.dtype),
             jax.ShapeDtypeStruct(momentum.shape, momentum.dtype),
         ],
-        in_specs=[smem] * 5 + [vmem] * (2 + len(operands)),
+        in_specs=[smem] * 4 + [vmem] * len(operands),
         out_specs=[vmem, vmem],
         scratch_shapes=[
             pltpu.VMEM((3, (rows + 16) * sub, LANES), jnp.float32),
             pltpu.VMEM((3, (rows + 4) * sub, LANES), jnp.float32),
             pltpu.VMEM((3, rows * sub, LANES), jnp.float32),
-        ],
+        ]
+        + [pltpu.VMEM((3, (rows + 16) * sub, LANES), jnp.float32)] * 4,
         compiler_params=pltpu.CompilerParams(vmem_limit_bytes=40 * 2**20),
-    )(shear_shift, shear_frac, advect_shift, advect_frac, rotation, density, momentum, *operands)
+    )(*kept, *operands)
 
 
 def solution(mesh):

time: 27.4 us -> 20 us (0.73)
  the two profiles are of different devices: /device:TPU:1 before, /device:TPU:0 now
where the time goes in v2:
time: 20 us; the launch traced here: 19.8 us
  starting transfers between devices  11.9 us (60%)
  Pallas kernels  3.71 us (19%)
  waiting for transfers between devices  2.83 us (14%)
  between operations  1.35 us (7%)
    ppermute x6, starting transfers between devices, across(): return lax.ppermute(value, 'az', [(i, i ^ away) for i in range(tiles)])  10.2 us
    pallas_call x1, Pallas kernels, per_device(): pl.pallas_call(functools.partial(step_kernel, (tiles, radials, rows, colu...  2.77 us
    ppermute x2, waiting for transfers between devices, swapped(): return lax.ppermute(value, 'rad', pairs + [(b, a) for a, b in pairs])  1.74 us
    ppermute x2, starting transfers between devices, swapped(): return lax.ppermute(value, 'rad', pairs + [(b, a) for a, b in pairs])  1.66 us
    ppermute x6, waiting for transfers between devices, across(): return lax.ppermute(value, 'az', [(i, i ^ away) for i in range(tiles)])  1.09 us
    pallas_call x1, Pallas kernels, per_device(): pl.pallas_call(split_kernel, out_shape=[pltpu.VMEM((3, 2 * HALO, columns)...  0.93 us
  transfers between devices with their start and end apart: 8, of which 3 were waited for; matrix products, arithmetic and copies ran while one was open for 0% of the time, Pallas kernels for 0%

profile of v2, /device:TPU:0, one launch (start us, length us, event | category | flops | bytes accessed | tf_op | source)
XLA Modules:
  0.0 19.8 jit_solution(17661816869633363076)
XLA Ops:
  0.6 0.9 %shard_map.86 = (f32[3,8,256]{2,1,0:T(8,128)S(1)}, f32[3,24,256]{2,1,0:T(8,128)S(1)}, s32[2]{0:T(128)S(4)}, f32[2]{0:T(128)S(4)}, s32[32]{0:T(128)S(4)}, /*index=5*/f32[32]{0:T(128)S(4)}) custom-call(s32[2]{0:T(128)} %refs_0_.1, f32[2]{0:T(128)} %refs_1_.1, s32[32]{0:T(128)} %refs_2_.1, f32[32]{0:T(128)} %refs_3_.1, f32[32,256]{1,0:T(8,128)} %refs_4_.1, ...), custom_call_target="tpu_custom_call" | custom-call | tf_op jit(solution)/shard_map/pallas_call | solution.py:451
  1.6 5.1 %collective-permute-start.2 = (f32[3,8,256]{2,1,0:T(8,128)S(1)}, f32[3,8,256]{2,1,0:T(8,128)S(1)}, u32[]{:S(2)}, u32[]{:S(2)}) collective-permute-start(f32[3,8,256]{2,1,0:T(8,128)S(1)} %get-tuple-element.12.refs_5_), channel_id=1, source_target_pairs={{0,12},{4,8},{8,4},{12,0},{1,13},{5,9},{9,5},{13,1},{2,14},{6,10},... | collective-permute-start | bytes 73736 | tf_op jit(solution)/shard_map/ppermute | solution.py:443
  6.7 0.0 collective-permute-start.1
  6.7 0.6 %collective-permute-start = (f32[3,8,256]{2,1,0:T(8,128)S(1)}, f32[3,8,256]{2,1,0:T(8,128)S(1)}, u32[]{:S(2)}, u32[]{:S(2)}) collective-permute-start(f32[3,8,256]{2,1,0:T(8,128)S(1)} %get-tuple-element.12.refs_5_), channel_id=1, source_target_pairs={{0,4},{4,0},{8,12},{12,8},{1,5},{5,1},{9,13},{13,9},{2,6},{6,2},{1... | collective-permute-start | bytes 73736 | tf_op jit(solution)/shard_map/ppermute | solution.py:443
  7.3 3.7 %collective-permute-start.5 = (f32[3,24,256]{2,1,0:T(8,128)S(1)}, f32[3,24,256]{2,1,0:T(8,128)S(1)}, u32[]{:S(2)}, u32[]{:S(2)}) collective-permute-start(f32[3,24,256]{2,1,0:T(8,128)S(1)} %get-tuple-element.13.refs_9_), channel_id=1, source_target_pairs={{0,12},{4,8},{8,4},{12,0},{1,13},{5,9},{9,5},{13,1},{2,14},{6,10},... | collective-permute-start | bytes 221192 | tf_op jit(solution)/shard_map/ppermute | solution.py:443
  11.1 0.0 collective-permute-start.4
  11.1 0.0 collective-permute-done.2.refs_8_
  11.1 0.7 %collective-permute-start.3 = (f32[3,24,256]{2,1,0:T(8,128)S(1)}, f32[3,24,256]{2,1,0:T(8,128)S(1)}, u32[]{:S(2)}, u32[]{:S(2)}) collective-permute-start(f32[3,24,256]{2,1,0:T(8,128)S(1)} %get-tuple-element.13.refs_9_), channel_id=1, source_target_pairs={{0,4},{4,0},{8,12},{12,8},{1,5},{5,1},{9,13},{13,9},{2,6},{6,2},{1... | collective-permute-start | bytes 221192 | tf_op jit(solution)/shard_map/ppermute | solution.py:443
  11.8 1.0 %collective-permute-done.1.refs_7_ = f32[3,8,256]{2,1,0:T(8,128)S(1)} collective-permute-done((f32[3,8,256]{2,1,0:T(8,128)S(1)}, f32[3,8,256]{2,1,0:T(8,128)S(1)}, u32[]{:S(2)}, u32[]{:S(2)}) %collective-permute-start.1) | collective-permute-done | bytes 24608 | tf_op jit(solution)/shard_map/ppermute | solution.py:443
  12.8 0.0 collective-permute-done.refs_6_
  12.9 0.1 collective-permute-start.7
  13.0 1.6 %collective-permute-start.6 = (f32[3,16,256]{2,1,0:T(8,128)S(1)}, f32[3,16,256]{2,1,0:T(8,128)S(1)}, u32[]{:S(2)}, u32[]{:S(2)}) collective-permute-start(f32[3,16,256]{2,1,0:T(8,128)S(1)} %get-tuple-element.15), channel_id=1, source_target_pairs={{0,1},{2,3},{1,0},{3,2},{4,5},{6,7},{5,4},{7,6},{8,9},{10,11},{9,8... | collective-permute-start | bytes 147464 | tf_op jit(solution)/shard_map/ppermute | solution.py:447
  15.2 1.7 %collective-permute-done.7.refs_14_ = f32[3,16,256]{2,1,0:T(8,128)S(1)} collective-permute-done((f32[3,16,256]{2,1,0:T(8,128)S(1)}, f32[3,16,256]{2,1,0:T(8,128)S(1)}, u32[]{:S(2)}, u32[]{:S(2)}) %collective-permute-start.7) | collective-permute-done | bytes 49184 | tf_op jit(solution)/shard_map/ppermute | solution.py:447
  16.9 0.0 collective-permute-done.6.refs_13_
  16.9 0.0 collective-permute-done.5.refs_12_
  16.9 0.1 collective-permute-done.4.refs_11_
  17.0 0.0 collective-permute-done.3.refs_10_
  17.0 2.8 %shard_map.87 = (f32[32,256]{1,0:T(8,128)}, f32[2,32,256]{2,1,0:T(8,128)}) custom-call(s32[2]{0:T(128)S(4)} %get-tuple-element.8.refs_0_, f32[2]{0:T(128)S(4)} %get-tuple-element.9.refs_1_, s32[32]{0:T(128)S(4)} %get-tuple-element.10.refs_2_, f32[32]{0:T(128)S(4)} %get-tuple-element.11.refs_3_, f32[8,128]{1,0:T(8,128)S(1)} %broadcast_in_dim.9.refs_4_, ...), custom_call_target="tpu_custom_call" | custom-call | tf_op jit(solution)/shard_map/pallas_call | solution.py:474
  (6 shorter events, 0.1 us)
Async XLA Ops:
  1.6 9.5 %collective-permute-start.2 = (f32[3,8,256]{2,1,0:T(8,128)S(1)}, f32[3,8,256]{2,1,0:T(8,128)S(1)}, u32[]{:S(2)}, u32[]{:S(2)}) collective-permute-start(f32[3,8,256]{2,1,0:T(8,128)S(1)} %get-tuple-element.12.refs_5_), channel_id=1, source_target_pairs={{0,12},{4,8},{8,4},{12,0},{1,13},{5,9},{9,5},{13,1},{2,14},{6,10},... | collective-permute-start | bytes 73736 | tf_op jit(solution)/shard_map/ppermute | solution.py:443
  6.7 6.1 %collective-permute-start.1 = (f32[3,8,256]{2,1,0:T(8,128)S(1)}, f32[3,8,256]{2,1,0:T(8,128)S(1)}, u32[]{:S(2)}, u32[]{:S(2)}) collective-permute-start(f32[3,8,256]{2,1,0:T(8,128)S(1)} %get-tuple-element.12.refs_5_), channel_id=1, source_target_pairs={{0,8},{4,12},{8,0},{12,4},{1,9},{5,13},{9,1},{13,5},{2,10},{6,14},... | collective-permute-start | bytes 73736 | tf_op jit(solution)/shard_map/ppermute | solution.py:443
  6.7 6.1 %collective-permute-start = (f32[3,8,256]{2,1,0:T(8,128)S(1)}, f32[3,8,256]{2,1,0:T(8,128)S(1)}, u32[]{:S(2)}, u32[]{:S(2)}) collective-permute-start(f32[3,8,256]{2,1,0:T(8,128)S(1)} %get-tuple-element.12.refs_5_), channel_id=1, source_target_pairs={{0,4},{4,0},{8,12},{12,8},{1,5},{5,1},{9,13},{13,9},{2,6},{6,2},{1... | collective-permute-start | bytes 73736 | tf_op jit(solution)/shard_map/ppermute | solution.py:443
  7.3 9.6 %collective-permute-start.5 = (f32[3,24,256]{2,1,0:T(8,128)S(1)}, f32[3,24,256]{2,1,0:T(8,128)S(1)}, u32[]{:S(2)}, u32[]{:S(2)}) collective-permute-start(f32[3,24,256]{2,1,0:T(8,128)S(1)} %get-tuple-element.13.refs_9_), channel_id=1, source_target_pairs={{0,12},{4,8},{8,4},{12,0},{1,13},{5,9},{9,5},{13,1},{2,14},{6,10},... | collective-permute-start | bytes 221192 | tf_op jit(solution)/shard_map/ppermute | solution.py:443
  11.1 5.9 %collective-permute-start.4 = (f32[3,24,256]{2,1,0:T(8,128)S(1)}, f32[3,24,256]{2,1,0:T(8,128)S(1)}, u32[]{:S(2)}, u32[]{:S(2)}) collective-permute-start(f32[3,24,256]{2,1,0:T(8,128)S(1)} %get-tuple-element.13.refs_9_), channel_id=1, source_target_pairs={{0,8},{4,12},{8,0},{12,4},{1,9},{5,13},{9,1},{13,5},{2,10},{6,14},... | collective-permute-start | bytes 221192 | tf_op jit(solution)/shard_map/ppermute | solution.py:443
  11.1 5.9 %collective-permute-start.3 = (f32[3,24,256]{2,1,0:T(8,128)S(1)}, f32[3,24,256]{2,1,0:T(8,128)S(1)}, u32[]{:S(2)}, u32[]{:S(2)}) collective-permute-start(f32[3,24,256]{2,1,0:T(8,128)S(1)} %get-tuple-element.13.refs_9_), channel_id=1, source_target_pairs={{0,4},{4,0},{8,12},{12,8},{1,5},{5,1},{9,13},{13,9},{2,6},{6,2},{1... | collective-permute-start | bytes 221192 | tf_op jit(solution)/shard_map/ppermute | solution.py:443
  12.9 4.1 %collective-permute-start.7 = (f32[3,16,256]{2,1,0:T(8,128)S(1)}, f32[3,16,256]{2,1,0:T(8,128)S(1)}, u32[]{:S(2)}, u32[]{:S(2)}) collective-permute-start(f32[3,16,256]{2,1,0:T(8,128)S(1)} %get-tuple-element.14), channel_id=1, source_target_pairs={{1,2},{3,0},{2,1},{0,3},{5,6},{7,4},{6,5},{4,7},{9,10},{11,8},{10,... | collective-permute-start | bytes 147464 | tf_op jit(solution)/shard_map/ppermute | solution.py:447
  13.0 4.0 %collective-permute-start.6 = (f32[3,16,256]{2,1,0:T(8,128)S(1)}, f32[3,16,256]{2,1,0:T(8,128)S(1)}, u32[]{:S(2)}, u32[]{:S(2)}) collective-permute-start(f32[3,16,256]{2,1,0:T(8,128)S(1)} %get-tuple-element.15), channel_id=1, source_target_pairs={{0,1},{2,3},{1,0},{3,2},{4,5},{6,7},{5,4},{7,6},{8,9},{10,11},{9,8... | collective-permute-start | bytes 147464 | tf_op jit(solution)/shard_map/ppermute | solution.py:447

commit v3 on v2

--- a/solution.py
+++ b/solution.py
@@ -116,8 +116,8 @@
 
 
 def split_kernel(*refs):
-    density, momentum, edges, inner = refs[4:8]
-    for given, kept in zip(refs[:4], refs[8:]):
+    advect_frac, density, momentum, edges, inner, weights = refs[3:9]
+    for given, kept in zip(refs[:3], refs[9:]):
         for place in range(given.shape[0]):
             kept[place] = given[place]
     rows = density.shape[0]
@@ -127,12 +127,14 @@
         edges[component, 0:HALO] = take(slice(0, HALO))
         edges[component, HALO : 2 * HALO] = take(slice(rows - HALO, rows))
         inner[component] = take(slice(HALO, rows - HALO))
+    for row in range(rows):
+        weights[row : row + 1, :] = jnp.full((1, LANES), advect_frac[row], jnp.float32)
 
 
 def step_kernel(sizes, *refs):
     tiles, radials, rows, columns, sub = sizes
     per_tile = columns // LANES
-    shear_shift, shear_frac, advect_shift, advect_frac, rotation = refs[:5]
+    shear_shift, shear_frac, advect_shift, weights, rotation = refs[:5]
     edges = refs[5 : 5 + tiles]
     inners = refs[5 + tiles : 5 + 2 * tiles]
     within, between, density_out, momentum_out, start, middle, remapped, whole, lower, upper, faces = refs[5 + 2 * tiles :]
@@ -250,11 +252,9 @@
     def emit_second(row, across):
         new = changed(state_of(middle, row), plus(across, turn(row)))
         old = state_of(start, row + main)
-        final = tuple(0.5 * o + 0.5 * n for o, n in zip(old, new))
+        final = tuple(0.5 * (o + n) for o, n in zip(old, new))
         shift = advect_shift[row - 2]
-        weight = advect_frac[row - 2]
-        moved = tuple(turned(f, shift // LANES, shift % LANES, lane) for f in final)
-        put(remapped, row - 2, tuple((1.0 - weight) * m + weight * previous(m, lane) for m in moved))
+        put(remapped, row - 2, tuple(turned(f, shift // LANES, shift % LANES, lane) for f in final))
 
     for row in (0, 1, rows + 2, rows + 3):
         only(middle, row)
@@ -262,12 +262,16 @@
     repeated(2, rows, LOOPS[1], meet)
     radial_sweep(lambda row: state_of(whole, row), emit_second, 2, rows, LOOPS[2])
 
-    for part in range(per_tile):
-        cut = slice(part * LANES, (part + 1) * LANES)
-        for row in range(0, rows, 8):
-            first = row * sub + az * per_tile + part
-            for component in range(3):
-                value = remapped[component, pl.ds(first, 8, stride=sub), :]
+    for row in range(0, rows, 8):
+        weight = weights[row : row + 8, :]
+        for component in range(3):
+            spots = [(az * per_tile + part + sub - 1) % sub for part in range(per_tile + 1)]
+            tiles_here = [remapped[component, pl.ds(row * sub + spot, 8, stride=sub), :] for spot in spots]
+            moved = [pltpu.roll(t, 1, 1) for t in tiles_here]
+            for part in range(per_tile):
+                cut = slice(part * LANES, (part + 1) * LANES)
+                before = jnp.where(lane == 0, moved[part], moved[part + 1])
+                value = (1.0 - weight) * tiles_here[part + 1] + weight * before
                 if component == 0:
                     density_out[row : row + 8, cut] = value
                 else:
@@ -448,15 +452,16 @@
 
     scalars = (shear_shift, shear_frac, advect_shift, advect_frac)
     spin = jnp.broadcast_to(rotation[:, None], (sub, LANES))
-    edge, inner, *kept = pl.pallas_call(
+    edge, inner, weights, *kept = pl.pallas_call(
         split_kernel,
         out_shape=[
             pltpu.VMEM((3, 2 * HALO, columns), jnp.float32),
             pltpu.VMEM((3, rows - 2 * HALO, columns), jnp.float32),
+            pltpu.VMEM((rows, LANES), jnp.float32),
         ]
-        + [pltpu.SMEM(s.shape, s.dtype) for s in scalars],
+        + [pltpu.SMEM(s.shape, s.dtype) for s in scalars[:3]],
         in_specs=[smem] * 4 + [vmem] * 2,
-        out_specs=[vmem] * 2 + [smem] * 4,
+        out_specs=[vmem] * 3 + [smem] * 3,
     )(*scalars, density, momentum)
     edges = {0: edge}
     inners = {0: inner}
@@ -467,22 +472,22 @@
     top = jnp.concatenate([edges[away][:, :HALO] for away in range(tiles)], axis=1)
     bottom = jnp.concatenate([edges[away][:, HALO:] for away in range(tiles)], axis=1)
     odd = lax.axis_index("rad") % 2 == 1
+    between = swapped(jnp.where(odd, bottom, top), 1)
     within = swapped(jnp.where(odd, top, bottom), 0)
-    between = swapped(jnp.where(odd, bottom, top), 1)
     operands = [edges[away] for away in range(tiles)] + [inners[away] for away in range(tiles)]
-    operands = [near(p) for p in [spin] + operands + [within, between]]
+    operands = [near(p) for p in [weights, spin] + operands + [within, between]]
     return pl.pallas_call(
         functools.partial(step_kernel, (tiles, radials, rows, columns, sub)),
         out_shape=[
             jax.ShapeDtypeStruct(density.shape, density.dtype),
             jax.ShapeDtypeStruct(momentum.shape, momentum.dtype),
         ],
-        in_specs=[smem] * 4 + [vmem] * len(operands),
+        in_specs=[smem] * 3 + [vmem] * len(operands),
         out_specs=[vmem, vmem],
         scratch_shapes=[
-            pltpu.VMEM((3, (rows + 16) * sub, LANES), jnp.float32),
+            pltpu.VMEM((3, (rows + 17) * sub, LANES), jnp.float32),
             pltpu.VMEM((3, (rows + 4) * sub, LANES), jnp.float32),
-            pltpu.VMEM((3, rows * sub, LANES), jnp.float32),
+            pltpu.VMEM((3, (rows + 1) * sub, LANES), jnp.float32),
         ]
         + [pltpu.VMEM((3, (rows + 16) * sub, LANES), jnp.float32)] * 4,
         compiler_params=pltpu.CompilerParams(vmem_limit_bytes=40 * 2**20),

time: 20 us -> 19.9 us (level)
  no operation moved by 1% of the time
where the time goes in v3:
time: 19.9 us; the launch traced here: 19.7 us
  starting transfers between devices  11.9 us (60%)
  Pallas kernels  3.6 us (18%)
  waiting for transfers between devices  2.83 us (14%)
  between operations  1.35 us (7%)
    ppermute x6, starting transfers between devices, across(): return lax.ppermute(value, 'az', [(i, i ^ away) for i in range(tiles)])  10.2 us
    pallas_call x1, Pallas kernels, per_device(): pl.pallas_call(functools.partial(step_kernel, (tiles, radials, rows, colu...  2.68 us
    ppermute x2, waiting for transfers between devices, swapped(): return lax.ppermute(value, 'rad', pairs + [(b, a) for a, b in pairs])  1.74 us
    ppermute x2, starting transfers between devices, swapped(): return lax.ppermute(value, 'rad', pairs + [(b, a) for a, b in pairs])  1.66 us
    ppermute x6, waiting for transfers between devices, across(): return lax.ppermute(value, 'az', [(i, i ^ away) for i in range(tiles)])  1.09 us
    pallas_call x1, Pallas kernels, per_device(): pl.pallas_call(split_kernel, out_shape=[pltpu.VMEM((3, 2 * HALO, columns)...  0.92 us
  transfers between devices with their start and end apart: 8, of which 3 were waited for; matrix products, arithmetic and copies ran while one was open for 0% of the time, Pallas kernels for 0%

profile of v3, /device:TPU:0, one launch (start us, length us, event | category | flops | bytes accessed | tf_op | source)
XLA Modules:
  0.0 19.7 jit_solution(10383313340235819395)
XLA Ops:
  0.6 0.9 %shard_map.86 = (f32[3,8,256]{2,1,0:T(8,128)S(1)}, f32[3,24,256]{2,1,0:T(8,128)S(1)}, f32[32,128]{1,0:T(8,128)S(1)}, s32[2]{0:T(128)S(4)}, f32[2]{0:T(128)S(4)}, /*index=5*/s32[32]{0:T(128)S(4)}) custom-call(s32[2]{0:T(128)} %refs_0_.1, f32[2]{0:T(128)} %refs_1_.1, s32[32]{0:T(128)} %refs_2_.1, f32[32]{0:T(128)} %refs_3_.1, f32[32,256]{1,0:T(8,128)} %refs_4_.1, ...), custom_call_target="tpu_custom_call" | custom-call | tf_op jit(solution)/shard_map/pallas_call | solution.py:455
  1.6 5.1 %collective-permute-start.2 = (f32[3,8,256]{2,1,0:T(8,128)S(1)}, f32[3,8,256]{2,1,0:T(8,128)S(1)}, u32[]{:S(2)}, u32[]{:S(2)}) collective-permute-start(f32[3,8,256]{2,1,0:T(8,128)S(1)} %get-tuple-element.12.refs_5_), channel_id=1, source_target_pairs={{0,12},{4,8},{8,4},{12,0},{1,13},{5,9},{9,5},{13,1},{2,14},{6,10},... | collective-permute-start | bytes 73736 | tf_op jit(solution)/shard_map/ppermute | solution.py:447
  6.7 0.0 collective-permute-start.1
  6.7 0.6 %collective-permute-start = (f32[3,8,256]{2,1,0:T(8,128)S(1)}, f32[3,8,256]{2,1,0:T(8,128)S(1)}, u32[]{:S(2)}, u32[]{:S(2)}) collective-permute-start(f32[3,8,256]{2,1,0:T(8,128)S(1)} %get-tuple-element.12.refs_5_), channel_id=1, source_target_pairs={{0,4},{4,0},{8,12},{12,8},{1,5},{5,1},{9,13},{13,9},{2,6},{6,2},{1... | collective-permute-start | bytes 73736 | tf_op jit(solution)/shard_map/ppermute | solution.py:447
  7.3 3.7 %collective-permute-start.5 = (f32[3,24,256]{2,1,0:T(8,128)S(1)}, f32[3,24,256]{2,1,0:T(8,128)S(1)}, u32[]{:S(2)}, u32[]{:S(2)}) collective-permute-start(f32[3,24,256]{2,1,0:T(8,128)S(1)} %get-tuple-element.13.refs_9_), channel_id=1, source_target_pairs={{0,12},{4,8},{8,4},{12,0},{1,13},{5,9},{9,5},{13,1},{2,14},{6,10},... | collective-permute-start | bytes 221192 | tf_op jit(solution)/shard_map/ppermute | solution.py:447
  11.1 0.0 collective-permute-start.4
  11.1 0.0 collective-permute-done.2.refs_8_
  11.1 0.7 %collective-permute-start.3 = (f32[3,24,256]{2,1,0:T(8,128)S(1)}, f32[3,24,256]{2,1,0:T(8,128)S(1)}, u32[]{:S(2)}, u32[]{:S(2)}) collective-permute-start(f32[3,24,256]{2,1,0:T(8,128)S(1)} %get-tuple-element.13.refs_9_), channel_id=1, source_target_pairs={{0,4},{4,0},{8,12},{12,8},{1,5},{5,1},{9,13},{13,9},{2,6},{6,2},{1... | collective-permute-start | bytes 221192 | tf_op jit(solution)/shard_map/ppermute | solution.py:447
  11.8 1.0 %collective-permute-done.1.refs_7_ = f32[3,8,256]{2,1,0:T(8,128)S(1)} collective-permute-done((f32[3,8,256]{2,1,0:T(8,128)S(1)}, f32[3,8,256]{2,1,0:T(8,128)S(1)}, u32[]{:S(2)}, u32[]{:S(2)}) %collective-permute-start.1) | collective-permute-done | bytes 24608 | tf_op jit(solution)/shard_map/ppermute | solution.py:447
  12.8 0.0 collective-permute-done.refs_6_
  12.9 0.1 collective-permute-start.7
  12.9 1.6 %collective-permute-start.6 = (f32[3,16,256]{2,1,0:T(8,128)S(1)}, f32[3,16,256]{2,1,0:T(8,128)S(1)}, u32[]{:S(2)}, u32[]{:S(2)}) collective-permute-start(f32[3,16,256]{2,1,0:T(8,128)S(1)} %get-tuple-element.15), channel_id=1, source_target_pairs={{0,1},{2,3},{1,0},{3,2},{4,5},{6,7},{5,4},{7,6},{8,9},{10,11},{9,8... | collective-permute-start | bytes 147464 | tf_op jit(solution)/shard_map/ppermute | solution.py:451
  15.2 1.7 %collective-permute-done.7.refs_14_ = f32[3,16,256]{2,1,0:T(8,128)S(1)} collective-permute-done((f32[3,16,256]{2,1,0:T(8,128)S(1)}, f32[3,16,256]{2,1,0:T(8,128)S(1)}, u32[]{:S(2)}, u32[]{:S(2)}) %collective-permute-start.7) | collective-permute-done | bytes 49184 | tf_op jit(solution)/shard_map/ppermute | solution.py:451
  16.9 0.0 collective-permute-done.6.refs_13_
  16.9 0.0 collective-permute-done.5.refs_12_
  16.9 0.1 collective-permute-done.4.refs_11_
  17.0 0.0 collective-permute-done.3.refs_10_
  17.0 2.7 %shard_map.87 = (f32[32,256]{1,0:T(8,128)}, f32[2,32,256]{2,1,0:T(8,128)}) custom-call(s32[2]{0:T(128)S(4)} %get-tuple-element.8.refs_0_, f32[2]{0:T(128)S(4)} %get-tuple-element.9.refs_1_, s32[32]{0:T(128)S(4)} %get-tuple-element.10.refs_2_, f32[32,128]{1,0:T(8,128)S(1)} %get-tuple-element.11.refs_3_, f32[8,128]{1,0:T(8,128)S(1)} %broadcast_in_dim.9.refs_4_, ...), custom_call_target="tpu_custom_call" | custom-call | tf_op jit(solution)/shard_map/pallas_call | solution.py:479
  (6 shorter events, 0.1 us)
Async XLA Ops:
  1.6 9.5 %collective-permute-start.2 = (f32[3,8,256]{2,1,0:T(8,128)S(1)}, f32[3,8,256]{2,1,0:T(8,128)S(1)}, u32[]{:S(2)}, u32[]{:S(2)}) collective-permute-start(f32[3,8,256]{2,1,0:T(8,128)S(1)} %get-tuple-element.12.refs_5_), channel_id=1, source_target_pairs={{0,12},{4,8},{8,4},{12,0},{1,13},{5,9},{9,5},{13,1},{2,14},{6,10},... | collective-permute-start | bytes 73736 | tf_op jit(solution)/shard_map/ppermute | solution.py:447
  6.7 6.1 %collective-permute-start.1 = (f32[3,8,256]{2,1,0:T(8,128)S(1)}, f32[3,8,256]{2,1,0:T(8,128)S(1)}, u32[]{:S(2)}, u32[]{:S(2)}) collective-permute-start(f32[3,8,256]{2,1,0:T(8,128)S(1)} %get-tuple-element.12.refs_5_), channel_id=1, source_target_pairs={{0,8},{4,12},{8,0},{12,4},{1,9},{5,13},{9,1},{13,5},{2,10},{6,14},... | collective-permute-start | bytes 73736 | tf_op jit(solution)/shard_map/ppermute | solution.py:447
  6.7 6.1 %collective-permute-start = (f32[3,8,256]{2,1,0:T(8,128)S(1)}, f32[3,8,256]{2,1,0:T(8,128)S(1)}, u32[]{:S(2)}, u32[]{:S(2)}) collective-permute-start(f32[3,8,256]{2,1,0:T(8,128)S(1)} %get-tuple-element.12.refs_5_), channel_id=1, source_target_pairs={{0,4},{4,0},{8,12},{12,8},{1,5},{5,1},{9,13},{13,9},{2,6},{6,2},{1... | collective-permute-start | bytes 73736 | tf_op jit(solution)/shard_map/ppermute | solution.py:447
  7.3 9.6 %collective-permute-start.5 = (f32[3,24,256]{2,1,0:T(8,128)S(1)}, f32[3,24,256]{2,1,0:T(8,128)S(1)}, u32[]{:S(2)}, u32[]{:S(2)}) collective-permute-start(f32[3,24,256]{2,1,0:T(8,128)S(1)} %get-tuple-element.13.refs_9_), channel_id=1, source_target_pairs={{0,12},{4,8},{8,4},{12,0},{1,13},{5,9},{9,5},{13,1},{2,14},{6,10},... | collective-permute-start | bytes 221192 | tf_op jit(solution)/shard_map/ppermute | solution.py:447
  11.1 5.9 %collective-permute-start.4 = (f32[3,24,256]{2,1,0:T(8,128)S(1)}, f32[3,24,256]{2,1,0:T(8,128)S(1)}, u32[]{:S(2)}, u32[]{:S(2)}) collective-permute-start(f32[3,24,256]{2,1,0:T(8,128)S(1)} %get-tuple-element.13.refs_9_), channel_id=1, source_target_pairs={{0,8},{4,12},{8,0},{12,4},{1,9},{5,13},{9,1},{13,5},{2,10},{6,14},... | collective-permute-start | bytes 221192 | tf_op jit(solution)/shard_map/ppermute | solution.py:447
  11.1 5.9 %collective-permute-start.3 = (f32[3,24,256]{2,1,0:T(8,128)S(1)}, f32[3,24,256]{2,1,0:T(8,128)S(1)}, u32[]{:S(2)}, u32[]{:S(2)}) collective-permute-start(f32[3,24,256]{2,1,0:T(8,128)S(1)} %get-tuple-element.13.refs_9_), channel_id=1, source_target_pairs={{0,4},{4,0},{8,12},{12,8},{1,5},{5,1},{9,13},{13,9},{2,6},{6,2},{1... | collective-permute-start | bytes 221192 | tf_op jit(solution)/shard_map/ppermute | solution.py:447
  12.9 4.1 %collective-permute-start.7 = (f32[3,16,256]{2,1,0:T(8,128)S(1)}, f32[3,16,256]{2,1,0:T(8,128)S(1)}, u32[]{:S(2)}, u32[]{:S(2)}) collective-permute-start(f32[3,16,256]{2,1,0:T(8,128)S(1)} %get-tuple-element.14), channel_id=1, source_target_pairs={{1,2},{3,0},{2,1},{0,3},{5,6},{7,4},{6,5},{4,7},{9,10},{11,8},{10,... | collective-permute-start | bytes 147464 | tf_op jit(solution)/shard_map/ppermute | solution.py:451
  12.9 4.0 %collective-permute-start.6 = (f32[3,16,256]{2,1,0:T(8,128)S(1)}, f32[3,16,256]{2,1,0:T(8,128)S(1)}, u32[]{:S(2)}, u32[]{:S(2)}) collective-permute-start(f32[3,16,256]{2,1,0:T(8,128)S(1)} %get-tuple-element.15), channel_id=1, source_target_pairs={{0,1},{2,3},{1,0},{3,2},{4,5},{6,7},{5,4},{7,6},{8,9},{10,11},{9,8... | collective-permute-start | bytes 147464 | tf_op jit(solution)/shard_map/ppermute | solution.py:451

commit v4 on v3

--- a/solution.py
+++ b/solution.py
@@ -135,8 +135,8 @@
     tiles, radials, rows, columns, sub = sizes
     per_tile = columns // LANES
     shear_shift, shear_frac, advect_shift, weights, rotation = refs[:5]
-    edges = refs[5 : 5 + tiles]
-    inners = refs[5 + tiles : 5 + 2 * tiles]
+    edges = dict(zip((0,) + EDGE_ORDER, refs[5 : 5 + tiles]))
+    inners = dict(zip((0,) + INNER_ORDER, refs[5 + tiles : 5 + 2 * tiles]))
     within, between, density_out, momentum_out, start, middle, remapped, whole, lower, upper, faces = refs[5 + 2 * tiles :]
     lane = lax.broadcasted_iota(jnp.int32, (sub, LANES), 1)
     az = lax.axis_index("az")
@@ -474,7 +474,8 @@
     odd = lax.axis_index("rad") % 2 == 1
     between = swapped(jnp.where(odd, bottom, top), 1)
     within = swapped(jnp.where(odd, top, bottom), 0)
-    operands = [edges[away] for away in range(tiles)] + [inners[away] for away in range(tiles)]
+    operands = [edges[away] for away in (0,) + EDGE_ORDER]
+    operands += [inners[away] for away in (0,) + INNER_ORDER]
     operands = [near(p) for p in [weights, spin] + operands + [within, between]]
     return pl.pallas_call(
         functools.partial(step_kernel, (tiles, radials, rows, columns, sub)),

time: 19.9 us -> 19 us (0.955)
  waiting for transfers between devices: 2.83 us -> 2.02 us
    ppermute x6, waiting for transfers between devices: 1.09 us -> 0.28 us  [across(): return lax.ppermute(value, 'az', [(i, i ^ away) for i in range(tiles)])]
  transfers between devices with their start and end apart: 8 -> 8, of which waited for: 3 -> 2; matrix products, arithmetic and copies ran while one was open for 0% -> 0% of each run, Pallas kernels for 0% -> 0%
where the time goes in v4:
time: 19 us; the launch traced here: 18.8 us
  starting transfers between devices  11.8 us (62%)
  Pallas kernels  3.6 us (19%)
  waiting for transfers between devices  2.02 us (11%)
  between operations  1.34 us (7%)
    ppermute x6, starting transfers between devices, across(): return lax.ppermute(value, 'az', [(i, i ^ away) for i in range(tiles)])  10.1 us
    pallas_call x1, Pallas kernels, per_device(): pl.pallas_call(functools.partial(step_kernel, (tiles, radials, rows, colu...  2.69 us
    ppermute x2, waiting for transfers between devices, swapped(): return lax.ppermute(value, 'rad', pairs + [(b, a) for a, b in pairs])  1.74 us
    ppermute x2, starting transfers between devices, swapped(): return lax.ppermute(value, 'rad', pairs + [(b, a) for a, b in pairs])  1.66 us
    pallas_call x1, Pallas kernels, per_device(): pl.pallas_call(split_kernel, out_shape=[pltpu.VMEM((3, 2 * HALO, columns)...  0.92 us
  transfers between devices with their start and end apart: 8, of which 2 were waited for; matrix products, arithmetic and copies ran while one was open for 0% of the time, Pallas kernels for 0%

profile of v4, /device:TPU:0, one launch (start us, length us, event | category | flops | bytes accessed | tf_op | source)
XLA Modules:
  0.0 18.8 jit_solution(13535878356638006815)
XLA Ops:
  0.6 0.9 %shard_map.86 = (f32[3,8,256]{2,1,0:T(8,128)S(1)}, f32[3,24,256]{2,1,0:T(8,128)S(1)}, f32[32,128]{1,0:T(8,128)S(1)}, s32[2]{0:T(128)S(4)}, f32[2]{0:T(128)S(4)}, /*index=5*/s32[32]{0:T(128)S(4)}) custom-call(s32[2]{0:T(128)} %refs_0_.1, f32[2]{0:T(128)} %refs_1_.1, s32[32]{0:T(128)} %refs_2_.1, f32[32]{0:T(128)} %refs_3_.1, f32[32,256]{1,0:T(8,128)} %refs_4_.1, ...), custom_call_target="tpu_custom_call" | custom-call | tf_op jit(solution)/shard_map/pallas_call | solution.py:455
  1.6 4.1 %collective-permute-start.2 = (f32[3,8,256]{2,1,0:T(8,128)S(1)}, f32[3,8,256]{2,1,0:T(8,128)S(1)}, u32[]{:S(2)}, u32[]{:S(2)}) collective-permute-start(f32[3,8,256]{2,1,0:T(8,128)S(1)} %get-tuple-element.12.refs_5_), channel_id=1, source_target_pairs={{0,8},{4,12},{8,0},{12,4},{1,9},{5,13},{9,1},{13,5},{2,10},{6,14},... | collective-permute-start | bytes 73736 | tf_op jit(solution)/shard_map/ppermute | solution.py:447
  5.7 1.3 %collective-permute-start.1 = (f32[3,8,256]{2,1,0:T(8,128)S(1)}, f32[3,8,256]{2,1,0:T(8,128)S(1)}, u32[]{:S(2)}, u32[]{:S(2)}) collective-permute-start(f32[3,8,256]{2,1,0:T(8,128)S(1)} %get-tuple-element.12.refs_5_), channel_id=1, source_target_pairs={{0,12},{4,8},{8,4},{12,0},{1,13},{5,9},{9,5},{13,1},{2,14},{6,10},... | collective-permute-start | bytes 73736 | tf_op jit(solution)/shard_map/ppermute | solution.py:447
  7.0 0.2 %collective-permute-start = (f32[3,8,256]{2,1,0:T(8,128)S(1)}, f32[3,8,256]{2,1,0:T(8,128)S(1)}, u32[]{:S(2)}, u32[]{:S(2)}) collective-permute-start(f32[3,8,256]{2,1,0:T(8,128)S(1)} %get-tuple-element.12.refs_5_), channel_id=1, source_target_pairs={{0,4},{4,0},{8,12},{12,8},{1,5},{5,1},{9,13},{13,9},{2,6},{6,2},{1... | collective-permute-start | bytes 73736 | tf_op jit(solution)/shard_map/ppermute | solution.py:447
  7.2 2.9 %collective-permute-start.5 = (f32[3,24,256]{2,1,0:T(8,128)S(1)}, f32[3,24,256]{2,1,0:T(8,128)S(1)}, u32[]{:S(2)}, u32[]{:S(2)}) collective-permute-start(f32[3,24,256]{2,1,0:T(8,128)S(1)} %get-tuple-element.13.refs_9_), channel_id=1, source_target_pairs={{0,12},{4,8},{8,4},{12,0},{1,13},{5,9},{9,5},{13,1},{2,14},{6,10},... | collective-permute-start | bytes 221192 | tf_op jit(solution)/shard_map/ppermute | solution.py:447
  10.2 0.5 %collective-permute-start.4 = (f32[3,24,256]{2,1,0:T(8,128)S(1)}, f32[3,24,256]{2,1,0:T(8,128)S(1)}, u32[]{:S(2)}, u32[]{:S(2)}) collective-permute-start(f32[3,24,256]{2,1,0:T(8,128)S(1)} %get-tuple-element.13.refs_9_), channel_id=1, source_target_pairs={{0,4},{4,0},{8,12},{12,8},{1,5},{5,1},{9,13},{13,9},{2,6},{6,2},{1... | collective-permute-start | bytes 221192 | tf_op jit(solution)/shard_map/ppermute | solution.py:447
  10.6 0.0 collective-permute-done.2.refs_8_
  10.6 1.1 %collective-permute-start.3 = (f32[3,24,256]{2,1,0:T(8,128)S(1)}, f32[3,24,256]{2,1,0:T(8,128)S(1)}, u32[]{:S(2)}, u32[]{:S(2)}) collective-permute-start(f32[3,24,256]{2,1,0:T(8,128)S(1)} %get-tuple-element.13.refs_9_), channel_id=1, source_target_pairs={{0,8},{4,12},{8,0},{12,4},{1,9},{5,13},{9,1},{13,5},{2,10},{6,14},... | collective-permute-start | bytes 221192 | tf_op jit(solution)/shard_map/ppermute | solution.py:447
  11.7 0.0 collective-permute-done.1.refs_7_
  11.7 0.0 collective-permute-done.refs_6_
  11.8 0.1 collective-permute-start.7
  11.9 1.6 %collective-permute-start.6 = (f32[3,16,256]{2,1,0:T(8,128)S(1)}, f32[3,16,256]{2,1,0:T(8,128)S(1)}, u32[]{:S(2)}, u32[]{:S(2)}) collective-permute-start(f32[3,16,256]{2,1,0:T(8,128)S(1)} %get-tuple-element.15), channel_id=1, source_target_pairs={{0,1},{2,3},{1,0},{3,2},{4,5},{6,7},{5,4},{7,6},{8,9},{10,11},{9,8... | collective-permute-start | bytes 147464 | tf_op jit(solution)/shard_map/ppermute | solution.py:451
  14.1 1.7 %collective-permute-done.7.refs_14_ = f32[3,16,256]{2,1,0:T(8,128)S(1)} collective-permute-done((f32[3,16,256]{2,1,0:T(8,128)S(1)}, f32[3,16,256]{2,1,0:T(8,128)S(1)}, u32[]{:S(2)}, u32[]{:S(2)}) %collective-permute-start.7) | collective-permute-done | bytes 49184 | tf_op jit(solution)/shard_map/ppermute | solution.py:451
  15.9 0.0 collective-permute-done.6.refs_13_
  15.9 0.0 collective-permute-done.5.refs_12_
  15.9 0.0 collective-permute-done.4.refs_11_
  15.9 0.3 %collective-permute-done.3.refs_10_ = f32[3,24,256]{2,1,0:T(8,128)S(1)} collective-permute-done((f32[3,24,256]{2,1,0:T(8,128)S(1)}, f32[3,24,256]{2,1,0:T(8,128)S(1)}, u32[]{:S(2)}, u32[]{:S(2)}) %collective-permute-start.3) | collective-permute-done | bytes 73760 | tf_op jit(solution)/shard_map/ppermute | solution.py:447
  16.1 2.7 %shard_map.87 = (f32[32,256]{1,0:T(8,128)}, f32[2,32,256]{2,1,0:T(8,128)}) custom-call(s32[2]{0:T(128)S(4)} %get-tuple-element.8.refs_0_, f32[2]{0:T(128)S(4)} %get-tuple-element.9.refs_1_, s32[32]{0:T(128)S(4)} %get-tuple-element.10.refs_2_, f32[32,128]{1,0:T(8,128)S(1)} %get-tuple-element.11.refs_3_, f32[8,128]{1,0:T(8,128)S(1)} %broadcast_in_dim.9.refs_4_, ...), custom_call_target="tpu_custom_call" | custom-call | tf_op jit(solution)/shard_map/pallas_call | solution.py:480
  (6 shorter events, 0.1 us)
Async XLA Ops:
  1.6 9.1 %collective-permute-start.2 = (f32[3,8,256]{2,1,0:T(8,128)S(1)}, f32[3,8,256]{2,1,0:T(8,128)S(1)}, u32[]{:S(2)}, u32[]{:S(2)}) collective-permute-start(f32[3,8,256]{2,1,0:T(8,128)S(1)} %get-tuple-element.12.refs_5_), channel_id=1, source_target_pairs={{0,8},{4,12},{8,0},{12,4},{1,9},{5,13},{9,1},{13,5},{2,10},{6,14},... | collective-permute-start | bytes 73736 | tf_op jit(solution)/shard_map/ppermute | solution.py:447
  5.7 6.1 %collective-permute-start.1 = (f32[3,8,256]{2,1,0:T(8,128)S(1)}, f32[3,8,256]{2,1,0:T(8,128)S(1)}, u32[]{:S(2)}, u32[]{:S(2)}) collective-permute-start(f32[3,8,256]{2,1,0:T(8,128)S(1)} %get-tuple-element.12.refs_5_), channel_id=1, source_target_pairs={{0,12},{4,8},{8,4},{12,0},{1,13},{5,9},{9,5},{13,1},{2,14},{6,10},... | collective-permute-start | bytes 73736 | tf_op jit(solution)/shard_map/ppermute | solution.py:447
  7.0 4.7 %collective-permute-start = (f32[3,8,256]{2,1,0:T(8,128)S(1)}, f32[3,8,256]{2,1,0:T(8,128)S(1)}, u32[]{:S(2)}, u32[]{:S(2)}) collective-permute-start(f32[3,8,256]{2,1,0:T(8,128)S(1)} %get-tuple-element.12.refs_5_), channel_id=1, source_target_pairs={{0,4},{4,0},{8,12},{12,8},{1,5},{5,1},{9,13},{13,9},{2,6},{6,2},{1... | collective-permute-start | bytes 73736 | tf_op jit(solution)/shard_map/ppermute | solution.py:447
  7.2 8.6 %collective-permute-start.5 = (f32[3,24,256]{2,1,0:T(8,128)S(1)}, f32[3,24,256]{2,1,0:T(8,128)S(1)}, u32[]{:S(2)}, u32[]{:S(2)}) collective-permute-start(f32[3,24,256]{2,1,0:T(8,128)S(1)} %get-tuple-element.13.refs_9_), channel_id=1, source_target_pairs={{0,12},{4,8},{8,4},{12,0},{1,13},{5,9},{9,5},{13,1},{2,14},{6,10},... | collective-permute-start | bytes 221192 | tf_op jit(solution)/shard_map/ppermute | solution.py:447
  10.2 5.7 %collective-permute-start.4 = (f32[3,24,256]{2,1,0:T(8,128)S(1)}, f32[3,24,256]{2,1,0:T(8,128)S(1)}, u32[]{:S(2)}, u32[]{:S(2)}) collective-permute-start(f32[3,24,256]{2,1,0:T(8,128)S(1)} %get-tuple-element.13.refs_9_), channel_id=1, source_target_pairs={{0,4},{4,0},{8,12},{12,8},{1,5},{5,1},{9,13},{13,9},{2,6},{6,2},{1... | collective-permute-start | bytes 221192 | tf_op jit(solution)/shard_map/ppermute | solution.py:447
  10.6 5.5 %collective-permute-start.3 = (f32[3,24,256]{2,1,0:T(8,128)S(1)}, f32[3,24,256]{2,1,0:T(8,128)S(1)}, u32[]{:S(2)}, u32[]{:S(2)}) collective-permute-start(f32[3,24,256]{2,1,0:T(8,128)S(1)} %get-tuple-element.13.refs_9_), channel_id=1, source_target_pairs={{0,8},{4,12},{8,0},{12,4},{1,9},{5,13},{9,1},{13,5},{2,10},{6,14},... | collective-permute-start | bytes 221192 | tf_op jit(solution)/shard_map/ppermute | solution.py:447
  11.8 4.1 %collective-permute-start.7 = (f32[3,16,256]{2,1,0:T(8,128)S(1)}, f32[3,16,256]{2,1,0:T(8,128)S(1)}, u32[]{:S(2)}, u32[]{:S(2)}) collective-permute-start(f32[3,16,256]{2,1,0:T(8,128)S(1)} %get-tuple-element.14), channel_id=1, source_target_pairs={{1,2},{3,0},{2,1},{0,3},{5,6},{7,4},{6,5},{4,7},{9,10},{11,8},{10,... | collective-permute-start | bytes 147464 | tf_op jit(solution)/shard_map/ppermute | solution.py:451
  11.9 4.0 %collective-permute-start.6 = (f32[3,16,256]{2,1,0:T(8,128)S(1)}, f32[3,16,256]{2,1,0:T(8,128)S(1)}, u32[]{:S(2)}, u32[]{:S(2)}) collective-permute-start(f32[3,16,256]{2,1,0:T(8,128)S(1)} %get-tuple-element.15), channel_id=1, source_target_pairs={{0,1},{2,3},{1,0},{3,2},{4,5},{6,7},{5,4},{7,6},{8,9},{10,11},{9,8... | collective-permute-start | bytes 147464 | tf_op jit(solution)/shard_map/ppermute | solution.py:451

commit v5 on v3

--- a/solution.py
+++ b/solution.py
@@ -135,8 +135,8 @@
     tiles, radials, rows, columns, sub = sizes
     per_tile = columns // LANES
     shear_shift, shear_frac, advect_shift, weights, rotation = refs[:5]
-    edges = refs[5 : 5 + tiles]
-    inners = refs[5 + tiles : 5 + 2 * tiles]
+    inners = dict(zip((0,) + INNER_ORDER, refs[5 : 5 + tiles]))
+    edges = dict(zip((0,) + EDGE_ORDER, refs[5 + tiles : 5 + 2 * tiles]))
     within, between, density_out, momentum_out, start, middle, remapped, whole, lower, upper, faces = refs[5 + 2 * tiles :]
     lane = lax.broadcasted_iota(jnp.int32, (sub, LANES), 1)
     az = lax.axis_index("az")
@@ -474,7 +474,8 @@
     odd = lax.axis_index("rad") % 2 == 1
     between = swapped(jnp.where(odd, bottom, top), 1)
     within = swapped(jnp.where(odd, top, bottom), 0)
-    operands = [edges[away] for away in range(tiles)] + [inners[away] for away in range(tiles)]
+    operands = [inners[away] for away in (0,) + INNER_ORDER]
+    operands += [edges[away] for away in (0,) + EDGE_ORDER]
     operands = [near(p) for p in [weights, spin] + operands + [within, between]]
     return pl.pallas_call(
         functools.partial(step_kernel, (tiles, radials, rows, columns, sub)),

time: 19.9 us -> 19 us (0.955)
  waiting for transfers between devices: 2.83 us -> 2.02 us
    ppermute x6, waiting for transfers between devices: 1.09 us -> 0.28 us  [across(): return lax.ppermute(value, 'az', [(i, i ^ away) for i in range(tiles)])]
  transfers between devices with their start and end apart: 8 -> 8, of which waited for: 3 -> 2; matrix products, arithmetic and copies ran while one was open for 0% -> 0% of each run, Pallas kernels for 0% -> 0%
where the time goes in v5:
time: 19 us; the launch traced here: 18.8 us
  starting transfers between devices  11.8 us (62%)
  Pallas kernels  3.61 us (19%)
  waiting for transfers between devices  2.02 us (11%)
  between operations  1.34 us (7%)
    ppermute x6, starting transfers between devices, across(): return lax.ppermute(value, 'az', [(i, i ^ away) for i in range(tiles)])  10.1 us
    pallas_call x1, Pallas kernels, per_device(): pl.pallas_call(functools.partial(step_kernel, (tiles, radials, rows, colu...  2.69 us
    ppermute x2, waiting for transfers between devices, swapped(): return lax.ppermute(value, 'rad', pairs + [(b, a) for a, b in pairs])  1.74 us
    ppermute x2, starting transfers between devices, swapped(): return lax.ppermute(value, 'rad', pairs + [(b, a) for a, b in pairs])  1.66 us
    pallas_call x1, Pallas kernels, per_device(): pl.pallas_call(split_kernel, out_shape=[pltpu.VMEM((3, 2 * HALO, columns)...  0.92 us
  transfers between devices with their start and end apart: 8, of which 2 were waited for; matrix products, arithmetic and copies ran while one was open for 0% of the time, Pallas kernels for 0%

profile of v5, /device:TPU:0, one launch (start us, length us, event | category | flops | bytes accessed | tf_op | source)
XLA Modules:
  0.0 18.8 jit_solution(5425913730401084554)
XLA Ops:
  0.6 0.9 %shard_map.86 = (f32[3,8,256]{2,1,0:T(8,128)S(1)}, f32[3,24,256]{2,1,0:T(8,128)S(1)}, f32[32,128]{1,0:T(8,128)S(1)}, s32[2]{0:T(128)S(4)}, f32[2]{0:T(128)S(4)}, /*index=5*/s32[32]{0:T(128)S(4)}) custom-call(s32[2]{0:T(128)} %refs_0_.1, f32[2]{0:T(128)} %refs_1_.1, s32[32]{0:T(128)} %refs_2_.1, f32[32]{0:T(128)} %refs_3_.1, f32[32,256]{1,0:T(8,128)} %refs_4_.1, ...), custom_call_target="tpu_custom_call" | custom-call | tf_op jit(solution)/shard_map/pallas_call | solution.py:455
  1.6 4.1 %collective-permute-start.5 = (f32[3,8,256]{2,1,0:T(8,128)S(1)}, f32[3,8,256]{2,1,0:T(8,128)S(1)}, u32[]{:S(2)}, u32[]{:S(2)}) collective-permute-start(f32[3,8,256]{2,1,0:T(8,128)S(1)} %get-tuple-element.13.refs_9_), channel_id=1, source_target_pairs={{0,8},{4,12},{8,0},{12,4},{1,9},{5,13},{9,1},{13,5},{2,10},{6,14},... | collective-permute-start | bytes 73736 | tf_op jit(solution)/shard_map/ppermute | solution.py:447
  5.7 1.3 %collective-permute-start.4 = (f32[3,8,256]{2,1,0:T(8,128)S(1)}, f32[3,8,256]{2,1,0:T(8,128)S(1)}, u32[]{:S(2)}, u32[]{:S(2)}) collective-permute-start(f32[3,8,256]{2,1,0:T(8,128)S(1)} %get-tuple-element.13.refs_9_), channel_id=1, source_target_pairs={{0,12},{4,8},{8,4},{12,0},{1,13},{5,9},{9,5},{13,1},{2,14},{6,10},... | collective-permute-start | bytes 73736 | tf_op jit(solution)/shard_map/ppermute | solution.py:447
  7.0 0.2 %collective-permute-start.3 = (f32[3,8,256]{2,1,0:T(8,128)S(1)}, f32[3,8,256]{2,1,0:T(8,128)S(1)}, u32[]{:S(2)}, u32[]{:S(2)}) collective-permute-start(f32[3,8,256]{2,1,0:T(8,128)S(1)} %get-tuple-element.13.refs_9_), channel_id=1, source_target_pairs={{0,4},{4,0},{8,12},{12,8},{1,5},{5,1},{9,13},{13,9},{2,6},{6,2},{1... | collective-permute-start | bytes 73736 | tf_op jit(solution)/shard_map/ppermute | solution.py:447
  7.2 2.9 %collective-permute-start.2 = (f32[3,24,256]{2,1,0:T(8,128)S(1)}, f32[3,24,256]{2,1,0:T(8,128)S(1)}, u32[]{:S(2)}, u32[]{:S(2)}) collective-permute-start(f32[3,24,256]{2,1,0:T(8,128)S(1)} %get-tuple-element.12.refs_5_), channel_id=1, source_target_pairs={{0,12},{4,8},{8,4},{12,0},{1,13},{5,9},{9,5},{13,1},{2,14},{6,10},... | collective-permute-start | bytes 221192 | tf_op jit(solution)/shard_map/ppermute | solution.py:447
  10.2 0.5 %collective-permute-start.1 = (f32[3,24,256]{2,1,0:T(8,128)S(1)}, f32[3,24,256]{2,1,0:T(8,128)S(1)}, u32[]{:S(2)}, u32[]{:S(2)}) collective-permute-start(f32[3,24,256]{2,1,0:T(8,128)S(1)} %get-tuple-element.12.refs_5_), channel_id=1, source_target_pairs={{0,4},{4,0},{8,12},{12,8},{1,5},{5,1},{9,13},{13,9},{2,6},{6,2},{1... | collective-permute-start | bytes 221192 | tf_op jit(solution)/shard_map/ppermute | solution.py:447
  10.6 0.0 collective-permute-done.5.refs_12_
  10.6 1.1 %collective-permute-start = (f32[3,24,256]{2,1,0:T(8,128)S(1)}, f32[3,24,256]{2,1,0:T(8,128)S(1)}, u32[]{:S(2)}, u32[]{:S(2)}) collective-permute-start(f32[3,24,256]{2,1,0:T(8,128)S(1)} %get-tuple-element.12.refs_5_), channel_id=1, source_target_pairs={{0,8},{4,12},{8,0},{12,4},{1,9},{5,13},{9,1},{13,5},{2,10},{6,14},... | collective-permute-start | bytes 221192 | tf_op jit(solution)/shard_map/ppermute | solution.py:447
  11.7 0.0 collective-permute-done.4.refs_11_
  11.7 0.0 collective-permute-done.3.refs_10_
  11.8 0.1 collective-permute-start.7
  11.9 1.6 %collective-permute-start.6 = (f32[3,16,256]{2,1,0:T(8,128)S(1)}, f32[3,16,256]{2,1,0:T(8,128)S(1)}, u32[]{:S(2)}, u32[]{:S(2)}) collective-permute-start(f32[3,16,256]{2,1,0:T(8,128)S(1)} %get-tuple-element.15), channel_id=1, source_target_pairs={{0,1},{2,3},{1,0},{3,2},{4,5},{6,7},{5,4},{7,6},{8,9},{10,11},{9,8... | collective-permute-start | bytes 147464 | tf_op jit(solution)/shard_map/ppermute | solution.py:451
  14.1 1.7 %collective-permute-done.7.refs_14_ = f32[3,16,256]{2,1,0:T(8,128)S(1)} collective-permute-done((f32[3,16,256]{2,1,0:T(8,128)S(1)}, f32[3,16,256]{2,1,0:T(8,128)S(1)}, u32[]{:S(2)}, u32[]{:S(2)}) %collective-permute-start.7) | collective-permute-done | bytes 49184 | tf_op jit(solution)/shard_map/ppermute | solution.py:451
  15.9 0.0 collective-permute-done.6.refs_13_
  15.9 0.0 collective-permute-done.2.refs_8_
  15.9 0.0 collective-permute-done.1.refs_7_
  15.9 0.3 %collective-permute-done.refs_6_ = f32[3,24,256]{2,1,0:T(8,128)S(1)} collective-permute-done((f32[3,24,256]{2,1,0:T(8,128)S(1)}, f32[3,24,256]{2,1,0:T(8,128)S(1)}, u32[]{:S(2)}, u32[]{:S(2)}) %collective-permute-start) | collective-permute-done | bytes 73760 | tf_op jit(solution)/shard_map/ppermute | solution.py:447
  16.1 2.7 %shard_map.87 = (f32[32,256]{1,0:T(8,128)}, f32[2,32,256]{2,1,0:T(8,128)}) custom-call(s32[2]{0:T(128)S(4)} %get-tuple-element.8.refs_0_, f32[2]{0:T(128)S(4)} %get-tuple-element.9.refs_1_, s32[32]{0:T(128)S(4)} %get-tuple-element.10.refs_2_, f32[32,128]{1,0:T(8,128)S(1)} %get-tuple-element.11.refs_3_, f32[8,128]{1,0:T(8,128)S(1)} %broadcast_in_dim.9.refs_4_, ...), custom_call_target="tpu_custom_call" | custom-call | tf_op jit(solution)/shard_map/pallas_call | solution.py:480
  (6 shorter events, 0.1 us)
Async XLA Ops:
  1.6 9.1 %collective-permute-start.5 = (f32[3,8,256]{2,1,0:T(8,128)S(1)}, f32[3,8,256]{2,1,0:T(8,128)S(1)}, u32[]{:S(2)}, u32[]{:S(2)}) collective-permute-start(f32[3,8,256]{2,1,0:T(8,128)S(1)} %get-tuple-element.13.refs_9_), channel_id=1, source_target_pairs={{0,8},{4,12},{8,0},{12,4},{1,9},{5,13},{9,1},{13,5},{2,10},{6,14},... | collective-permute-start | bytes 73736 | tf_op jit(solution)/shard_map/ppermute | solution.py:447
  5.7 6.1 %collective-permute-start.4 = (f32[3,8,256]{2,1,0:T(8,128)S(1)}, f32[3,8,256]{2,1,0:T(8,128)S(1)}, u32[]{:S(2)}, u32[]{:S(2)}) collective-permute-start(f32[3,8,256]{2,1,0:T(8,128)S(1)} %get-tuple-element.13.refs_9_), channel_id=1, source_target_pairs={{0,12},{4,8},{8,4},{12,0},{1,13},{5,9},{9,5},{13,1},{2,14},{6,10},... | collective-permute-start | bytes 73736 | tf_op jit(solution)/shard_map/ppermute | solution.py:447
  7.0 4.7 %collective-permute-start.3 = (f32[3,8,256]{2,1,0:T(8,128)S(1)}, f32[3,8,256]{2,1,0:T(8,128)S(1)}, u32[]{:S(2)}, u32[]{:S(2)}) collective-permute-start(f32[3,8,256]{2,1,0:T(8,128)S(1)} %get-tuple-element.13.refs_9_), channel_id=1, source_target_pairs={{0,4},{4,0},{8,12},{12,8},{1,5},{5,1},{9,13},{13,9},{2,6},{6,2},{1... | collective-permute-start | bytes 73736 | tf_op jit(solution)/shard_map/ppermute | solution.py:447
  7.2 8.6 %collective-permute-start.2 = (f32[3,24,256]{2,1,0:T(8,128)S(1)}, f32[3,24,256]{2,1,0:T(8,128)S(1)}, u32[]{:S(2)}, u32[]{:S(2)}) collective-permute-start(f32[3,24,256]{2,1,0:T(8,128)S(1)} %get-tuple-element.12.refs_5_), channel_id=1, source_target_pairs={{0,12},{4,8},{8,4},{12,0},{1,13},{5,9},{9,5},{13,1},{2,14},{6,10},... | collective-permute-start | bytes 221192 | tf_op jit(solution)/shard_map/ppermute | solution.py:447
  10.2 5.7 %collective-permute-start.1 = (f32[3,24,256]{2,1,0:T(8,128)S(1)}, f32[3,24,256]{2,1,0:T(8,128)S(1)}, u32[]{:S(2)}, u32[]{:S(2)}) collective-permute-start(f32[3,24,256]{2,1,0:T(8,128)S(1)} %get-tuple-element.12.refs_5_), channel_id=1, source_target_pairs={{0,4},{4,0},{8,12},{12,8},{1,5},{5,1},{9,13},{13,9},{2,6},{6,2},{1... | collective-permute-start | bytes 221192 | tf_op jit(solution)/shard_map/ppermute | solution.py:447
  10.6 5.5 %collective-permute-start = (f32[3,24,256]{2,1,0:T(8,128)S(1)}, f32[3,24,256]{2,1,0:T(8,128)S(1)}, u32[]{:S(2)}, u32[]{:S(2)}) collective-permute-start(f32[3,24,256]{2,1,0:T(8,128)S(1)} %get-tuple-element.12.refs_5_), channel_id=1, source_target_pairs={{0,8},{4,12},{8,0},{12,4},{1,9},{5,13},{9,1},{13,5},{2,10},{6,14},... | collective-permute-start | bytes 221192 | tf_op jit(solution)/shard_map/ppermute | solution.py:447
  11.8 4.1 %collective-permute-start.7 = (f32[3,16,256]{2,1,0:T(8,128)S(1)}, f32[3,16,256]{2,1,0:T(8,128)S(1)}, u32[]{:S(2)}, u32[]{:S(2)}) collective-permute-start(f32[3,16,256]{2,1,0:T(8,128)S(1)} %get-tuple-element.14), channel_id=1, source_target_pairs={{1,2},{3,0},{2,1},{0,3},{5,6},{7,4},{6,5},{4,7},{9,10},{11,8},{10,... | collective-permute-start | bytes 147464 | tf_op jit(solution)/shard_map/ppermute | solution.py:451
  11.9 4.0 %collective-permute-start.6 = (f32[3,16,256]{2,1,0:T(8,128)S(1)}, f32[3,16,256]{2,1,0:T(8,128)S(1)}, u32[]{:S(2)}, u32[]{:S(2)}) collective-permute-start(f32[3,16,256]{2,1,0:T(8,128)S(1)} %get-tuple-element.15), channel_id=1, source_target_pairs={{0,1},{2,3},{1,0},{3,2},{4,5},{6,7},{5,4},{7,6},{8,9},{10,11},{9,8... | collective-permute-start | bytes 147464 | tf_op jit(solution)/shard_map/ppermute | solution.py:451
